TPU v7x, 512 devices: a whole 4x4x16 slice. The times are simulated.
512 devices in a mesh: row: 32 (over z, x_lo), col: 16 (over x_hi, y, core).
Axes of the slice: x: 4 (x_hi: 2, x_lo: 2; x = x_hi * 2 + x_lo), y: 4, z: 16, core: 2. Of those that a mesh axis runs over, the one named last changes fastest.
Arguments:
- queries: bfloat16 [96, 1024, 128], P('row', 'col'), may hold values from -8 to 8
- keys: bfloat16 [96, 1024, 128], P('row', 'col'), may hold values from -8 to 8
- values: bfloat16 [96, 1024, 128], P('row', 'col'), may hold values from -6 to 6
- pair_mask: int32 [96, 1024], P('row', 'col'), may hold values 0 or 1
- tri_bias: bfloat16 [4, 1024, 1024], P(None, ('col', 'row')), may hold values from -8 to 400
- grad_out: bfloat16 [96, 1024, 128], P('row', 'col'), may hold values from -20 to 20
Outputs:
- query_grad: bfloat16 [96, 1024, 128], P('row', 'col')
- key_grad: bfloat16 [96, 1024, 128], P('row', 'col')
- value_grad: bfloat16 [96, 1024, 128], P('row', 'col')
- bias_grad: float32 [4, 1024, 1024], P(None, ('col', 'row'))
All inputs are finite; a program needn't handle non-finite values. No bound on the sum of `pair_mask` on one device may be relied on, other than what follows from the above.
Results may differ from a plain program's by a relative error of at most 0.0051.
Values may be sent and summed in bfloat16 or wider, within the bound.
A program may use at most 64 MiB of HBM per device.

v0:
```python
import jax
import jax.numpy as jnp
from jax import lax
from jax.sharding import PartitionSpec as P


def shifted(block, axis, distance):
    devices = range(lax.axis_size(axis))
    route = [((i - distance) % len(devices), i) for i in devices]
    return lax.ppermute(block, axis, route)


def on_device(queries, keys, values, pair_mask, tri_bias, grad_out):
    row_count, col_count, width = queries.shape
    head_count = tri_bias.shape[0]
    head_size = width // head_count
    score_scale = head_size ** (-0.5)
    cycle_length = lax.axis_size("col")
    cycle_place = lax.axis_index("col")
    bias_rows = lax.all_gather(tri_bias, "row", axis=1, tiled=True)
    query_heads = queries.reshape(row_count, col_count, head_count, head_size)
    grad_heads = grad_out.reshape(row_count, col_count, head_count, head_size)

    def tile_scores(key_tile, mask_tile, source_block):
        key_heads = key_tile.reshape(row_count, col_count, head_count, head_size)
        raw = jnp.einsum(
            "rjhe,rkhe->rhjk", query_heads, key_heads, preferred_element_type=jnp.float32
        )
        bias_tile = lax.dynamic_slice_in_dim(
            bias_rows, source_block * col_count, col_count, 2
        ).astype(jnp.float32)
        penalty = 1000000000.0 * (mask_tile.astype(jnp.float32) - 1.0)
        return raw * score_scale + bias_tile[None] + penalty[:, None, None, :]

    def tile_dots(value_tile):
        value_heads = value_tile.reshape(row_count, col_count, head_count, head_size)
        return jnp.einsum(
            "rjhe,rkhe->rhjk", grad_heads, value_heads, preferred_element_type=jnp.float32
        )

    def stats_turn(source_block, key_tile, value_tile, mask_tile, stats):
        maximum, total_mass, weighted = stats
        scores = tile_scores(key_tile, mask_tile, source_block)
        prob_grads = tile_dots(value_tile)
        new_maximum = jnp.maximum(maximum, jnp.max(scores, axis=-1))
        factor = jnp.exp(maximum - new_maximum)
        expo = jnp.exp(scores - new_maximum[..., None])
        total_mass = total_mass * factor + jnp.sum(expo, axis=-1)
        weighted = weighted * factor + jnp.sum(expo * prob_grads, axis=-1)
        return (new_maximum, total_mass, weighted)

    def grads_turn(
        source_block, key_tile, value_tile, mask_tile, maximum, total_mass, delta, state
    ):
        query_grads, key_grads, value_grads, bias_grads = state
        scores = tile_scores(key_tile, mask_tile, source_block)
        probs = jnp.exp(scores - maximum[..., None]) / total_mass[..., None]
        prob_grads = tile_dots(value_tile)
        score_grads = probs * (prob_grads - delta[..., None])
        probs_low = probs.astype(jnp.bfloat16)
        score_low = score_grads.astype(jnp.bfloat16)
        key_heads = key_tile.reshape(row_count, col_count, head_count, head_size)
        query_grads = query_grads + jnp.einsum(
            "rhjk,rkhe->rjhe", score_low, key_heads, preferred_element_type=jnp.float32
        ).reshape(row_count, col_count, width)
        key_grads = key_grads + jnp.einsum(
            "rhjk,rjhe->rkhe", score_low, query_heads, preferred_element_type=jnp.float32
        ).reshape(row_count, col_count, width)
        value_grads = value_grads + jnp.einsum(
            "rhjk,rjhe->rkhe", probs_low, grad_heads, preferred_element_type=jnp.float32
        ).reshape(row_count, col_count, width)
        bias_grads = lax.dynamic_update_slice_in_dim(
            bias_grads, jnp.sum(score_grads, axis=0), source_block * col_count, 2
        )
        key_grads, value_grads = shifted((key_grads, value_grads), "col", 1)
        return (query_grads, key_grads, value_grads, bias_grads)

    stat_shape = (row_count, head_count, col_count)
    start_stats = (
        jnp.full(stat_shape, -1e30, jnp.float32),
        jnp.zeros(stat_shape, jnp.float32),
        jnp.zeros(stat_shape, jnp.float32),
    )
    grad_zeros = jnp.zeros((row_count, col_count, width), jnp.float32)
    start_state = (
        grad_zeros,
        grad_zeros,
        grad_zeros,
        jnp.zeros((head_count, col_count, col_count * cycle_length), jnp.float32),
    )
    all_keys, all_values, all_mask = (
        lax.all_gather(keys, "col", axis=1, tiled=True),
        lax.all_gather(values, "col", axis=1, tiled=True),
        lax.all_gather(pair_mask, "col", axis=1, tiled=True),
    )

    def pick_tile(source_block):
        offset = source_block * col_count
        return (
            lax.dynamic_slice_in_dim(all_keys, offset, col_count, 1),
            lax.dynamic_slice_in_dim(all_values, offset, col_count, 1),
            lax.dynamic_slice_in_dim(all_mask, offset, col_count, 1),
        )

    def first_loop(cycle_step, stats):
        source_block = (cycle_place - cycle_step) % cycle_length
        key_tile, value_tile, mask_tile = pick_tile(source_block)
        return stats_turn(source_block, key_tile, value_tile, mask_tile, stats)

    maximum, total_mass, weighted = lax.fori_loop(0, cycle_length, first_loop, start_stats)
    delta = weighted / total_mass

    def second_loop(cycle_step, state):
        source_block = (cycle_place - cycle_step) % cycle_length
        key_tile, value_tile, mask_tile = pick_tile(source_block)
        return grads_turn(
            source_block, key_tile, value_tile, mask_tile, maximum, total_mass, delta, state
        )

    final_state = lax.fori_loop(0, cycle_length, second_loop, start_state)
    query_grads, key_grads, value_grads, bias_grads = final_state
    bias_out = lax.psum_scatter(bias_grads, "row", scatter_dimension=1, tiled=True)
    return (
        (score_scale * query_grads).astype(jnp.bfloat16),
        (score_scale * key_grads).astype(jnp.bfloat16),
        value_grads.astype(jnp.bfloat16),
        bias_out,
    )


def solution(mesh):
    return jax.shard_map(
        on_device,
        mesh=mesh,
        in_specs=(
            P("row", "col", None),
            P("row", "col", None),
            P("row", "col", None),
            P("row", "col"),
            P(None, ("col", "row"), None),
            P("row", "col", None),
        ),
        out_specs=(
            P("row", "col", None),
            P("row", "col", None),
            P("row", "col", None),
            P(None, ("col", "row"), None),
        ),
        check_vma=False,
    )
```

profile of v0, /device:TPU:24, one launch (start us, length us, event | category | flops | bytes accessed | tf_op | source)
XLA Modules:
  0.0 748.4 jit_solution(3726930858118266589)
XLA Ops:
  7.3 22.7 %all_gather.12 = bf16[3,1024,128]{2,1,0:T(8,128)(2,1)S(1)} all-gather(bf16[3,64,128]{2,1,0:T(8,128)(2,1)} %param.11), channel_id=1, replica_groups=mesh['row'=32,'col'=16] {'col'}, dimensions={1}, use_global_device_ids=true | all-gather | bytes 835584 | tf_op jit(solution)/shard_map/all_gather | solution.py:92
  31.5 69.5 %all_gather.13 = bf16[4,64,1024]{2,0,1:T(4,128)(2,1)S(1)} all-gather(bf16[4,2,1024]{2,0,1:T(4,128)(2,1)S(1)} %copy.43), channel_id=1, replica_groups=mesh['row'=32,'col'=16] {'row'}, dimensions={1}, use_global_device_ids=true | all-gather | bytes 540672 | tf_op jit(solution)/shard_map/all_gather | solution.py:20
  101.0 1.4 copy.50
  102.3 22.4 %all-gather = s32[16,64,3]{1,2,0:T(4,128)S(1)} all-gather(s32[1,64,3]{1,2,0:T(4,128)S(1)} %bitcast.118), channel_id=1, replica_groups=mesh['row'=32,'col'=16] {'col'}, dimensions={0}, use_global_device_ids=true | all-gather | bytes 13056 | tf_op jit(solution)/shard_map/all_gather | solution.py:94
  125.6 21.1 %all_gather.15 = bf16[3,1024,128]{2,1,0:T(8,128)(2,1)S(1)} all-gather(bf16[3,64,128]{2,1,0:T(8,128)(2,1)S(1)} %copy-done.1), channel_id=1, replica_groups=mesh['row'=32,'col'=16] {'col'}, dimensions={1}, use_global_device_ids=true | all-gather | bytes 835584 | tf_op jit(solution)/shard_map/all_gather | solution.py:93
  146.7 1.2 copy.48
  148.0 43.6 %while.42 = (s32[]{:T(128)}, f32[3,4,64]{2,1,0:T(4,128)S(1)}, f32[3,4,64]{2,1,0:T(4,128)S(1)}, f32[3,4,64]{2,1,0:T(4,128)S(1)}, s32[]{:T(128)}, /*index=5*/bf16[...) while((s32[]{:T(128)}, f32[3,4,64]{2,1,0:T(4,128)S(1)}, ...), condition=%wide.region_4.5_spmd.clone, body=%wide.region_0.4_spmd.clone.sunk | while | flops 6756179 | bytes 1204835 | solution.py:110
  191.9 285.9 %while.43 = (s32[]{:T(128)}, f32[3,64,128]{1,2,0:T(8,128)S(1)}, f32[3,64,128]{1,2,0:T(8,128)S(1)}, f32[3,64,128]{1,2,0:T(8,128)S(1)}, f32[4,64,1024]{2,0,1:T(4,1...) while((s32[]{:T(128)}, f32[3,64,128]{1,2,0:T(8,128)S(1)}, ...), condition=%wide.region_7.8_spmd.clone, body=%wide.region_5.7_spmd.clone.sunk | while | flops 16319059 | bytes 3894994 | solution.py:120
  194.8 2.3 collective-permute-start
  197.4 7.3 collective-permute-start.1
  205.0 1.0 dynamic_update_slice.12
  209.0 10.9 %collective-permute-start = (f32[3,64,128]{1,2,0:T(8,128)S(1)}, f32[3,64,128]{1,2,0:T(8,128)S(1)}, u32[]{:S(2)}, u32[]{:S(2)}) collective-permute-start(f32[3,64,128]{1,2,0:T(8,128)S(1)} %bitcast_add_fusion.7), channel_id=1, source_target_pairs={{15,0},{0,1},{1,2},{2,3},{3,4},{4,5},{5,6},{6,7},{7,8},{8,9},{9,10... | collective-permute-start | bytes 294920 | tf_op jit(solution)/shard_map/while/body/eval_jaxpr/ppermute | solution.py:10
  220.1 1.9 collective-permute-start.1
  222.4 9.7 %dynamic_update_slice.12 = f32[4,64,1024]{2,0,1:T(4,128)S(1)} dynamic-update-slice(f32[4,64,1024]{2,0,1:T(4,128)S(1)} %get-tuple-element.1094, f32[4,64,64]{2,0,1:T(4,128)S(1)} %copy.63, s32[]{:T(128)} %constant.214.clone.1..sunk.1, s32[]{:T(128)} %constant.214.clone.1..sunk.1, s32[]{:T(128)S(6)} %select_n.75) | dynamic-update-slice | bytes 131076 | tf_op jit(solution)/shard_map/while/body/eval_jaxpr/dynamic_update_slice | solution.py:72
  235.0 1.9 collective-permute-start
  237.2 2.1 collective-permute-start.1
  239.6 1.0 dynamic_update_slice.12
  240.7 1.4 collective-permute-done
  242.0 2.2 collective-permute-done.1
  247.1 7.1 collective-permute-start
  254.4 1.9 collective-permute-start.1
  256.7 9.7 %dynamic_update_slice.12 = f32[4,64,1024]{2,0,1:T(4,128)S(1)} dynamic-update-slice(f32[4,64,1024]{2,0,1:T(4,128)S(1)} %get-tuple-element.1094, f32[4,64,64]{2,0,1:T(4,128)S(1)} %copy.63, s32[]{:T(128)} %constant.214.clone.1..sunk.1, s32[]{:T(128)} %constant.214.clone.1..sunk.1, s32[]{:T(128)S(6)} %select_n.75) | dynamic-update-slice | bytes 131076 | tf_op jit(solution)/shard_map/while/body/eval_jaxpr/dynamic_update_slice | solution.py:72
  269.3 1.9 collective-permute-start
  271.5 1.9 collective-permute-start.1
  274.8 1.5 collective-permute-done
  276.3 2.2 collective-permute-done.1
  281.4 6.9 collective-permute-start
  288.6 1.9 collective-permute-start.1
  290.9 9.7 %dynamic_update_slice.12 = f32[4,64,1024]{2,0,1:T(4,128)S(1)} dynamic-update-slice(f32[4,64,1024]{2,0,1:T(4,128)S(1)} %get-tuple-element.1094, f32[4,64,64]{2,0,1:T(4,128)S(1)} %copy.63, s32[]{:T(128)} %constant.214.clone.1..sunk.1, s32[]{:T(128)} %constant.214.clone.1..sunk.1, s32[]{:T(128)S(6)} %select_n.75) | dynamic-update-slice | bytes 131076 | tf_op jit(solution)/shard_map/while/body/eval_jaxpr/dynamic_update_slice | solution.py:72
  303.5 1.9 collective-permute-start
  305.7 2.2 collective-permute-start.1
  309.3 1.2 collective-permute-done
  310.5 2.2 collective-permute-done.1
  315.5 7.2 collective-permute-start
  323.0 1.9 collective-permute-start.1
  325.3 9.6 %dynamic_update_slice.12 = f32[4,64,1024]{2,0,1:T(4,128)S(1)} dynamic-update-slice(f32[4,64,1024]{2,0,1:T(4,128)S(1)} %get-tuple-element.1094, f32[4,64,64]{2,0,1:T(4,128)S(1)} %copy.63, s32[]{:T(128)} %constant.214.clone.1..sunk.1, s32[]{:T(128)} %constant.214.clone.1..sunk.1, s32[]{:T(128)S(6)} %select_n.75) | dynamic-update-slice | bytes 131076 | tf_op jit(solution)/shard_map/while/body/eval_jaxpr/dynamic_update_slice | solution.py:72
  337.8 1.9 collective-permute-start
  340.0 7.6 %collective-permute-start.1 = (f32[3,64,128]{1,2,0:T(8,128)S(1)}, f32[3,64,128]{1,2,0:T(8,128)S(1)}, u32[]{:S(2)}, u32[]{:S(2)}) collective-permute-start(f32[3,64,128]{1,2,0:T(8,128)S(1)} %bitcast_add_fusion.8), channel_id=1, source_target_pairs={{15,0},{0,1},{1,2},{2,3},{3,4},{4,5},{5,6},{6,7},{7,8},{8,9},{9,10... | collective-permute-start | bytes 294920 | tf_op jit(solution)/shard_map/while/body/eval_jaxpr/ppermute | solution.py:10
  351.9 10.5 %collective-permute-start = (f32[3,64,128]{1,2,0:T(8,128)S(1)}, f32[3,64,128]{1,2,0:T(8,128)S(1)}, u32[]{:S(2)}, u32[]{:S(2)}) collective-permute-start(f32[3,64,128]{1,2,0:T(8,128)S(1)} %bitcast_add_fusion.7), channel_id=1, source_target_pairs={{15,0},{0,1},{1,2},{2,3},{3,4},{4,5},{5,6},{6,7},{7,8},{8,9},{9,10... | collective-permute-start | bytes 294920 | tf_op jit(solution)/shard_map/while/body/eval_jaxpr/ppermute | solution.py:10
  362.7 1.9 collective-permute-start.1
  365.0 9.7 %dynamic_update_slice.12 = f32[4,64,1024]{2,0,1:T(4,128)S(1)} dynamic-update-slice(f32[4,64,1024]{2,0,1:T(4,128)S(1)} %get-tuple-element.1094, f32[4,64,64]{2,0,1:T(4,128)S(1)} %copy.63, s32[]{:T(128)} %constant.214.clone.1..sunk.1, s32[]{:T(128)} %constant.214.clone.1..sunk.1, s32[]{:T(128)S(6)} %select_n.75) | dynamic-update-slice | bytes 131076 | tf_op jit(solution)/shard_map/while/body/eval_jaxpr/dynamic_update_slice | solution.py:72
  377.6 1.9 collective-permute-start
  379.8 2.1 collective-permute-start.1
  382.2 1.0 dynamic_update_slice.12
  383.3 1.4 collective-permute-done
  384.6 2.2 collective-permute-done.1
  389.7 7.1 collective-permute-start
  397.0 1.9 collective-permute-start.1
  399.3 9.7 %dynamic_update_slice.12 = f32[4,64,1024]{2,0,1:T(4,128)S(1)} dynamic-update-slice(f32[4,64,1024]{2,0,1:T(4,128)S(1)} %get-tuple-element.1094, f32[4,64,64]{2,0,1:T(4,128)S(1)} %copy.63, s32[]{:T(128)} %constant.214.clone.1..sunk.1, s32[]{:T(128)} %constant.214.clone.1..sunk.1, s32[]{:T(128)S(6)} %select_n.75) | dynamic-update-slice | bytes 131076 | tf_op jit(solution)/shard_map/while/body/eval_jaxpr/dynamic_update_slice | solution.py:72
  411.9 1.9 collective-permute-start
  414.1 1.9 collective-permute-start.1
  417.4 1.5 collective-permute-done
  418.9 2.2 collective-permute-done.1
  424.0 6.9 collective-permute-start
  431.2 1.9 collective-permute-start.1
  433.5 9.7 %dynamic_update_slice.12 = f32[4,64,1024]{2,0,1:T(4,128)S(1)} dynamic-update-slice(f32[4,64,1024]{2,0,1:T(4,128)S(1)} %get-tuple-element.1094, f32[4,64,64]{2,0,1:T(4,128)S(1)} %copy.63, s32[]{:T(128)} %constant.214.clone.1..sunk.1, s32[]{:T(128)} %constant.214.clone.1..sunk.1, s32[]{:T(128)S(6)} %select_n.75) | dynamic-update-slice | bytes 131076 | tf_op jit(solution)/shard_map/while/body/eval_jaxpr/dynamic_update_slice | solution.py:72
  446.1 1.9 collective-permute-start
  448.3 2.4 collective-permute-start.1
  453.1 2.2 collective-permute-done.1
  458.1 7.5 collective-permute-start
  465.9 1.9 collective-permute-start.1
  468.1 9.7 %dynamic_update_slice.12 = f32[4,64,1024]{2,0,1:T(4,128)S(1)} dynamic-update-slice(f32[4,64,1024]{2,0,1:T(4,128)S(1)} %get-tuple-element.1094, f32[4,64,64]{2,0,1:T(4,128)S(1)} %copy.63, s32[]{:T(128)} %constant.214.clone.1..sunk.1, s32[]{:T(128)} %constant.214.clone.1..sunk.1, s32[]{:T(128)S(6)} %select_n.75) | dynamic-update-slice | bytes 131076 | tf_op jit(solution)/shard_map/while/body/eval_jaxpr/dynamic_update_slice | solution.py:72
  479.8 1.3 dynamic-slice
  482.4 257.8 %all-reduce.3.cloned.1.call-done = f32[4,64,1024]{2,0,1:T(4,128)} async-done(((f32[4,64,1024]{2,0,1:T(4,128)}), f32[4,64,1024]{2,0,1:T(4,128)}) %all-reduce.3.cloned.1.call-update) | async-done | bytes 1048592
  (412 shorter events, 110.1 us)
Async XLA Ops:
  7.2 733.0 %all-reduce.3.cloned.1.call-start = ((), (), s32[]{:S(2)}) async-start(), calls=%async_computation | async-start | bytes 2097152
  29.9 0.8 copy-start.2
  30.7 0.7 copy-start.4
  100.9 1.4 copy-start.5
  124.8 0.8 copy-start.1
  146.7 1.2 copy-start.3
  194.8 11.2 %collective-permute-start = (f32[3,64,128]{1,2,0:T(8,128)S(1)}, f32[3,64,128]{1,2,0:T(8,128)S(1)}, u32[]{:S(2)}, u32[]{:S(2)}) collective-permute-start(f32[3,64,128]{1,2,0:T(8,128)S(1)} %bitcast_add_fusion.7), channel_id=1, source_target_pairs={{15,0},{0,1},{1,2},{2,3},{3,4},{4,5},{5,6},{6,7},{7,8},{8,9},{9,10... | collective-permute-start | bytes 294920 | tf_op jit(solution)/shard_map/while/body/eval_jaxpr/ppermute | solution.py:10
  197.4 8.7 %collective-permute-start.1 = (f32[3,64,128]{1,2,0:T(8,128)S(1)}, f32[3,64,128]{1,2,0:T(8,128)S(1)}, u32[]{:S(2)}, u32[]{:S(2)}) collective-permute-start(f32[3,64,128]{1,2,0:T(8,128)S(1)} %bitcast_add_fusion.8), channel_id=1, source_target_pairs={{15,0},{0,1},{1,2},{2,3},{3,4},{4,5},{5,6},{6,7},{7,8},{8,9},{9,10... | collective-permute-start | bytes 294920 | tf_op jit(solution)/shard_map/while/body/eval_jaxpr/ppermute | solution.py:10
  209.0 23.1 %collective-permute-start = (f32[3,64,128]{1,2,0:T(8,128)S(1)}, f32[3,64,128]{1,2,0:T(8,128)S(1)}, u32[]{:S(2)}, u32[]{:S(2)}) collective-permute-start(f32[3,64,128]{1,2,0:T(8,128)S(1)} %bitcast_add_fusion.7), channel_id=1, source_target_pairs={{15,0},{0,1},{1,2},{2,3},{3,4},{4,5},{5,6},{6,7},{7,8},{8,9},{9,10... | collective-permute-start | bytes 294920 | tf_op jit(solution)/shard_map/while/body/eval_jaxpr/ppermute | solution.py:10
  220.1 12.0 %collective-permute-start.1 = (f32[3,64,128]{1,2,0:T(8,128)S(1)}, f32[3,64,128]{1,2,0:T(8,128)S(1)}, u32[]{:S(2)}, u32[]{:S(2)}) collective-permute-start(f32[3,64,128]{1,2,0:T(8,128)S(1)} %bitcast_add_fusion.8), channel_id=1, source_target_pairs={{15,0},{0,1},{1,2},{2,3},{3,4},{4,5},{5,6},{6,7},{7,8},{8,9},{9,10... | collective-permute-start | bytes 294920 | tf_op jit(solution)/shard_map/while/body/eval_jaxpr/ppermute | solution.py:10
  235.0 7.0 collective-permute-start
  237.2 7.0 collective-permute-start.1
  247.1 19.3 %collective-permute-start = (f32[3,64,128]{1,2,0:T(8,128)S(1)}, f32[3,64,128]{1,2,0:T(8,128)S(1)}, u32[]{:S(2)}, u32[]{:S(2)}) collective-permute-start(f32[3,64,128]{1,2,0:T(8,128)S(1)} %bitcast_add_fusion.7), channel_id=1, source_target_pairs={{15,0},{0,1},{1,2},{2,3},{3,4},{4,5},{5,6},{6,7},{7,8},{8,9},{9,10... | collective-permute-start | bytes 294920 | tf_op jit(solution)/shard_map/while/body/eval_jaxpr/ppermute | solution.py:10
  254.4 12.0 %collective-permute-start.1 = (f32[3,64,128]{1,2,0:T(8,128)S(1)}, f32[3,64,128]{1,2,0:T(8,128)S(1)}, u32[]{:S(2)}, u32[]{:S(2)}) collective-permute-start(f32[3,64,128]{1,2,0:T(8,128)S(1)} %bitcast_add_fusion.8), channel_id=1, source_target_pairs={{15,0},{0,1},{1,2},{2,3},{3,4},{4,5},{5,6},{6,7},{7,8},{8,9},{9,10... | collective-permute-start | bytes 294920 | tf_op jit(solution)/shard_map/while/body/eval_jaxpr/ppermute | solution.py:10
  269.3 7.0 collective-permute-start
  271.5 7.0 collective-permute-start.1
  281.4 19.1 %collective-permute-start = (f32[3,64,128]{1,2,0:T(8,128)S(1)}, f32[3,64,128]{1,2,0:T(8,128)S(1)}, u32[]{:S(2)}, u32[]{:S(2)}) collective-permute-start(f32[3,64,128]{1,2,0:T(8,128)S(1)} %bitcast_add_fusion.7), channel_id=1, source_target_pairs={{15,0},{0,1},{1,2},{2,3},{3,4},{4,5},{5,6},{6,7},{7,8},{8,9},{9,10... | collective-permute-start | bytes 294920 | tf_op jit(solution)/shard_map/while/body/eval_jaxpr/ppermute | solution.py:10
  288.6 12.0 %collective-permute-start.1 = (f32[3,64,128]{1,2,0:T(8,128)S(1)}, f32[3,64,128]{1,2,0:T(8,128)S(1)}, u32[]{:S(2)}, u32[]{:S(2)}) collective-permute-start(f32[3,64,128]{1,2,0:T(8,128)S(1)} %bitcast_add_fusion.8), channel_id=1, source_target_pairs={{15,0},{0,1},{1,2},{2,3},{3,4},{4,5},{5,6},{6,7},{7,8},{8,9},{9,10... | collective-permute-start | bytes 294920 | tf_op jit(solution)/shard_map/while/body/eval_jaxpr/ppermute | solution.py:10
  303.5 7.0 collective-permute-start
  305.7 7.0 collective-permute-start.1
  315.5 19.3 %collective-permute-start = (f32[3,64,128]{1,2,0:T(8,128)S(1)}, f32[3,64,128]{1,2,0:T(8,128)S(1)}, u32[]{:S(2)}, u32[]{:S(2)}) collective-permute-start(f32[3,64,128]{1,2,0:T(8,128)S(1)} %bitcast_add_fusion.7), channel_id=1, source_target_pairs={{15,0},{0,1},{1,2},{2,3},{3,4},{4,5},{5,6},{6,7},{7,8},{8,9},{9,10... | collective-permute-start | bytes 294920 | tf_op jit(solution)/shard_map/while/body/eval_jaxpr/ppermute | solution.py:10
  323.0 11.9 %collective-permute-start.1 = (f32[3,64,128]{1,2,0:T(8,128)S(1)}, f32[3,64,128]{1,2,0:T(8,128)S(1)}, u32[]{:S(2)}, u32[]{:S(2)}) collective-permute-start(f32[3,64,128]{1,2,0:T(8,128)S(1)} %bitcast_add_fusion.8), channel_id=1, source_target_pairs={{15,0},{0,1},{1,2},{2,3},{3,4},{4,5},{5,6},{6,7},{7,8},{8,9},{9,10... | collective-permute-start | bytes 294920 | tf_op jit(solution)/shard_map/while/body/eval_jaxpr/ppermute | solution.py:10
  337.8 11.1 %collective-permute-start = (f32[3,64,128]{1,2,0:T(8,128)S(1)}, f32[3,64,128]{1,2,0:T(8,128)S(1)}, u32[]{:S(2)}, u32[]{:S(2)}) collective-permute-start(f32[3,64,128]{1,2,0:T(8,128)S(1)} %bitcast_add_fusion.7), channel_id=1, source_target_pairs={{15,0},{0,1},{1,2},{2,3},{3,4},{4,5},{5,6},{6,7},{7,8},{8,9},{9,10... | collective-permute-start | bytes 294920 | tf_op jit(solution)/shard_map/while/body/eval_jaxpr/ppermute | solution.py:10
  340.0 8.9 %collective-permute-start.1 = (f32[3,64,128]{1,2,0:T(8,128)S(1)}, f32[3,64,128]{1,2,0:T(8,128)S(1)}, u32[]{:S(2)}, u32[]{:S(2)}) collective-permute-start(f32[3,64,128]{1,2,0:T(8,128)S(1)} %bitcast_add_fusion.8), channel_id=1, source_target_pairs={{15,0},{0,1},{1,2},{2,3},{3,4},{4,5},{5,6},{6,7},{7,8},{8,9},{9,10... | collective-permute-start | bytes 294920 | tf_op jit(solution)/shard_map/while/body/eval_jaxpr/ppermute | solution.py:10
  351.9 22.7 %collective-permute-start = (f32[3,64,128]{1,2,0:T(8,128)S(1)}, f32[3,64,128]{1,2,0:T(8,128)S(1)}, u32[]{:S(2)}, u32[]{:S(2)}) collective-permute-start(f32[3,64,128]{1,2,0:T(8,128)S(1)} %bitcast_add_fusion.7), channel_id=1, source_target_pairs={{15,0},{0,1},{1,2},{2,3},{3,4},{4,5},{5,6},{6,7},{7,8},{8,9},{9,10... | collective-permute-start | bytes 294920 | tf_op jit(solution)/shard_map/while/body/eval_jaxpr/ppermute | solution.py:10
  362.7 12.0 %collective-permute-start.1 = (f32[3,64,128]{1,2,0:T(8,128)S(1)}, f32[3,64,128]{1,2,0:T(8,128)S(1)}, u32[]{:S(2)}, u32[]{:S(2)}) collective-permute-start(f32[3,64,128]{1,2,0:T(8,128)S(1)} %bitcast_add_fusion.8), channel_id=1, source_target_pairs={{15,0},{0,1},{1,2},{2,3},{3,4},{4,5},{5,6},{6,7},{7,8},{8,9},{9,10... | collective-permute-start | bytes 294920 | tf_op jit(solution)/shard_map/while/body/eval_jaxpr/ppermute | solution.py:10
  377.6 7.0 collective-permute-start
  379.8 7.0 collective-permute-start.1
  389.7 19.3 %collective-permute-start = (f32[3,64,128]{1,2,0:T(8,128)S(1)}, f32[3,64,128]{1,2,0:T(8,128)S(1)}, u32[]{:S(2)}, u32[]{:S(2)}) collective-permute-start(f32[3,64,128]{1,2,0:T(8,128)S(1)} %bitcast_add_fusion.7), channel_id=1, source_target_pairs={{15,0},{0,1},{1,2},{2,3},{3,4},{4,5},{5,6},{6,7},{7,8},{8,9},{9,10... | collective-permute-start | bytes 294920 | tf_op jit(solution)/shard_map/while/body/eval_jaxpr/ppermute | solution.py:10
  397.0 12.0 %collective-permute-start.1 = (f32[3,64,128]{1,2,0:T(8,128)S(1)}, f32[3,64,128]{1,2,0:T(8,128)S(1)}, u32[]{:S(2)}, u32[]{:S(2)}) collective-permute-start(f32[3,64,128]{1,2,0:T(8,128)S(1)} %bitcast_add_fusion.8), channel_id=1, source_target_pairs={{15,0},{0,1},{1,2},{2,3},{3,4},{4,5},{5,6},{6,7},{7,8},{8,9},{9,10... | collective-permute-start | bytes 294920 | tf_op jit(solution)/shard_map/while/body/eval_jaxpr/ppermute | solution.py:10
  411.9 7.0 collective-permute-start
  414.1 7.0 collective-permute-start.1
  424.0 19.1 %collective-permute-start = (f32[3,64,128]{1,2,0:T(8,128)S(1)}, f32[3,64,128]{1,2,0:T(8,128)S(1)}, u32[]{:S(2)}, u32[]{:S(2)}) collective-permute-start(f32[3,64,128]{1,2,0:T(8,128)S(1)} %bitcast_add_fusion.7), channel_id=1, source_target_pairs={{15,0},{0,1},{1,2},{2,3},{3,4},{4,5},{5,6},{6,7},{7,8},{8,9},{9,10... | collective-permute-start | bytes 294920 | tf_op jit(solution)/shard_map/while/body/eval_jaxpr/ppermute | solution.py:10
  431.2 12.0 %collective-permute-start.1 = (f32[3,64,128]{1,2,0:T(8,128)S(1)}, f32[3,64,128]{1,2,0:T(8,128)S(1)}, u32[]{:S(2)}, u32[]{:S(2)}) collective-permute-start(f32[3,64,128]{1,2,0:T(8,128)S(1)} %bitcast_add_fusion.8), channel_id=1, source_target_pairs={{15,0},{0,1},{1,2},{2,3},{3,4},{4,5},{5,6},{6,7},{7,8},{8,9},{9,10... | collective-permute-start | bytes 294920 | tf_op jit(solution)/shard_map/while/body/eval_jaxpr/ppermute | solution.py:10
  446.1 7.0 collective-permute-start
  448.3 7.0 collective-permute-start.1
  458.1 19.7 %collective-permute-start = (f32[3,64,128]{1,2,0:T(8,128)S(1)}, f32[3,64,128]{1,2,0:T(8,128)S(1)}, u32[]{:S(2)}, u32[]{:S(2)}) collective-permute-start(f32[3,64,128]{1,2,0:T(8,128)S(1)} %bitcast_add_fusion.7), channel_id=1, source_target_pairs={{15,0},{0,1},{1,2},{2,3},{3,4},{4,5},{5,6},{6,7},{7,8},{8,9},{9,10... | collective-permute-start | bytes 294920 | tf_op jit(solution)/shard_map/while/body/eval_jaxpr/ppermute | solution.py:10
  465.9 12.0 %collective-permute-start.1 = (f32[3,64,128]{1,2,0:T(8,128)S(1)}, f32[3,64,128]{1,2,0:T(8,128)S(1)}, u32[]{:S(2)}, u32[]{:S(2)}) collective-permute-start(f32[3,64,128]{1,2,0:T(8,128)S(1)} %bitcast_add_fusion.8), channel_id=1, source_target_pairs={{15,0},{0,1},{1,2},{2,3},{3,4},{4,5},{5,6},{6,7},{7,8},{8,9},{9,10... | collective-permute-start | bytes 294920 | tf_op jit(solution)/shard_map/while/body/eval_jaxpr/ppermute | solution.py:10
  477.8 1.0 copy-start
Sparse Core Ops, SparseCore 0:
  479.0 261.1 all-reduce.2
where the time goes:
time: 752 us; the launch traced here: 748 us
  waiting for transfers between devices  279 us (37%)
  blocking collectives  136 us (18%)
  local copies, waits for them, and re-layouts  131 us (17%)
  starting transfers between devices  123 us (16%)
  other arithmetic  34.9 us (5%)
  matrix products  27.4 us (4%)
  between operations  14.8 us (2%)
    unnamed x2, waiting for transfers between devices  258 us
    ppermute x32, starting transfers between devices, shifted(): return lax.ppermute(block, axis, route)  123 us
    dynamic_update_slice x32, local copies, waits for them, and re-layouts, grads_turn(): lax.dynamic_update_slice_in_dim(bias_grads, jnp.sum(score_grads, axis=0),...  87.1 us
    all_gather x1, blocking collectives, on_device(): bias_rows = lax.all_gather(tri_bias, 'row', axis=1, tiled=True)  69.5 us
    dynamic_slice x32, local copies, waits for them, and re-layouts, pick_tile(): lax.dynamic_slice_in_dim(all_values, offset, col_count, 1)  32.2 us
    convert_element_type x32, other arithmetic, tile_scores(): bias_tile = lax.dynamic_slice_in_dim(bias_rows, source_block * col_count,...  27.2 us
    all_gather x1, blocking collectives, on_device(): lax.all_gather(keys, 'col', axis=1, tiled=True)  22.7 us
    all_gather x1, blocking collectives, on_device(): lax.all_gather(pair_mask, 'col', axis=1, tiled=True)  22.4 us
  transfers between devices with their start and end apart: 33, of which 13 were waited for; matrix products, arithmetic and copies ran while one was open for 13% of the time, Pallas kernels for 0%

commit v1 on v0

v1 whole, which is shorter than its diff:
```python
import functools

import jax
import jax.numpy as jnp
from jax import lax
from jax.experimental import pallas as pl
from jax.experimental.pallas import tpu as pltpu
from jax.sharding import PartitionSpec as P

MESH = pl.DeviceIdType.MESH
F32, BF16 = jnp.float32, jnp.bfloat16
SCALE = 32 ** -0.5
ROWS = 3
NT = (((1,), (1,)), ((), ()))
TN = (((0,), (0,)), ((), ()))


def iota(shape, dim):
    return lax.broadcasted_iota(jnp.int32, shape, dim)


def dot(a, b):
    return jnp.dot(a, b, preferred_element_type=F32)


def zero_one(hit):
    return jnp.where(hit, 1.0, 0.0).astype(BF16)


def class_place(at):
    return ((at >> 1) & 3) * 16 + (at >> 4) * 4 + ((at >> 3) & 1) * 2 + (at & 1)


def swap_place(at):
    return ((at >> 5) & 3) * 128 + (at >> 7) * 32 + (at & 31)


def half_place(at):
    return ((at >> 5) & 1) * 128 + (at >> 6) * 32 + (at & 31)


def kernel(
    q_ref, k_ref, v_ref, mask_ref, bias_ref, do_ref,
    dq_ref, dk_ref, dv_ref, dbias_ref,
    swap, kv_send, kv_recv, kv_roll, pen, qd_send, qd_recv, lhs, b_wide, b_send, b_all, b_f32,
    d_f32, d_send, d_recv, d_sum, e_recv, dkv_t, dkv_send, dkv_recv, dq_buf, dq_send, dq_recv,
    kv_ss, kv_rs, qd_ss, qd_rs, b1_ss, b1_rs, b2_ss, b2_rs,
    d2_ss, d2_rs, e_ss, e_rs, dkv_ss, dkv_rs, dq_ss, dq_rs,
):
    r, c = lax.axis_index("row"), lax.axis_index("col")
    z, xl = r // 2, r % 2
    y = (c // 2) % 4
    zq, kappa = z // 4, z % 4

    def at_z(dz, dxl):
        return ((z + dz + 16) % 16) * 2 + (xl + dxl) % 2

    def at_y(dy):
        return c + (((y + dy) % 4) - y) * 2

    def yz(o):
        dy, dz = o // 4, (o % 4) * 4
        return (y + dy) % 4, ((z + dz) % 16) // 4, (at_z(dz, 0), at_y(dy))

    def copy(src, dst, ss, rs, device):
        return pltpu.make_async_remote_copy(
            src_ref=src, dst_ref=dst, send_sem=ss, recv_sem=rs, device_id=device, device_id_type=MESH
        )

    def each(low, high, do):
        def body(o, carry):
            do(o)
            return carry

        lax.fori_loop(low, high, body, 0)

    near = [(0, 1)] + [(dz, dxl) for dz in (1, -1, 2, -2) for dxl in (0, 1)]
    barrier = pltpu.get_barrier_semaphore()

    def greet(device):
        pl.semaphore_signal(barrier, inc=1, device_id=device, device_id_type=MESH)

    def greet_yz(o):
        dy, dz = o % 4, (o // 4) * 4
        greet((at_z(dz, 0), at_y(dy)))

    each(4, 16, greet_yz)
    each(1, 16, lambda o: greet((r, (c + o) % 16)))
    for dz, dxl in near:
        greet((at_z(dz, dxl), c))

    wide = jnp.concatenate([bias_ref[h] for h in range(4)], axis=0)
    half_mat = zero_one(half_place(iota((256, 256), 0)) == iota((256, 256), 1))
    for m in range(4):
        turned = dot(wide[:, 256 * m:256 * (m + 1)], half_mat)
        for half in range(2):
            b_wide[pl.ds(half * 4 + m, 8, stride=8), :] = turned[:, 128 * half:128 * (half + 1)]
    b_send[...] = b_wide[...].astype(BF16).reshape(4, 16, 128)

    swap_mat = zero_one(swap_place(iota((512, 512), 0)) == iota((512, 512), 1))
    swap[...] = swap_mat
    spread = swap_mat[:256] + swap_mat[256:]
    low_lanes = iota((32, 128), 1) < 64
    mask_lane = (iota((8, 128), 1) >> 5) == c % 4
    mask = mask_ref[...].astype(F32)
    tiles = []
    for half in range(2):
        part = mask[:, 32 * half:32 * (half + 1)]
        part = jnp.concatenate([part] * 4, axis=1)
        part = jnp.concatenate([part, jnp.zeros((8 - ROWS, 128), F32)], axis=0)
        tiles.append(jnp.where(mask_lane, part, 0.0))
    mask_tile = jnp.concatenate(tiles, axis=0).astype(BF16)
    for h in range(4):
        kv_send[h, 96:112, :] = mask_tile
    for i in range(ROWS):
        pairs = dot(jnp.concatenate([k_ref[i], v_ref[i]], axis=1), spread)
        for h in range(4):
            one = pairs[:, 128 * h:128 * (h + 1)]
            kv_send[h, 32 * i:32 * (i + 1), :] = jnp.where(low_lanes, one[:32], one[32:]).astype(BF16)
    order = zero_one(class_place(iota((64, 64), 0)) == iota((64, 64), 1))
    low8 = iota((8, 128), 1) < 64
    for i in range(ROWS):
        turned = dot(order, jnp.concatenate([q_ref[i], do_ref[i]], axis=1)).astype(BF16)
        pairs = dot(turned, spread)
        for h in range(4):
            one = pairs[:, 128 * h:128 * (h + 1)]
            parts = [jnp.where(low8, one[16 * a:16 * a + 8], one[16 * a + 8:16 * a + 16]) for a in range(4)]
            qd_send[h, 32 * i:32 * (i + 1), :] = jnp.concatenate(parts, axis=0).astype(BF16)

    pl.semaphore_wait(barrier, 12 + 15 + len(near))

    def b1(o):
        to_y, _, device = yz(o)
        return copy(b_send.at[to_y], b_all.at[kappa, xl, y * 4 + zq], b1_ss.at[o], b1_rs.at[o], device)

    def kv(o):
        to = (c + o) % 16
        return copy(kv_send.at[(to // 2) % 4], kv_recv.at[c], kv_ss.at[o], kv_rs.at[o], (r, to))

    def qd(o):
        return copy(qd_send.at[(y + o) % 4], qd_recv.at[y], qd_ss.at[o], qd_rs.at[o], (r, at_y(o)))

    each(1, 16, lambda o: b1(o).start())
    each(1, 4, lambda o: qd(o).start())
    each(1, 16, lambda o: kv(o).start())
    b_all[kappa, xl, y * 4 + zq] = b_send[y]
    kv_recv[c] = kv_send[y]
    qd_recv[y] = qd_send[y]

    each(1, 16, lambda o: b1(o).wait_recv())

    def b2(j):
        dz, dxl = near[j]
        mine = b_all.at[kappa, xl]
        if dz == 2:
            mine = mine.at[pl.ds(0, 8)]
        elif dz == -2:
            mine = mine.at[pl.ds(8, 8)]
        return copy(mine, mine, b2_ss.at[j], b2_rs.at[j], (at_z(dz, dxl), c))

    for j in range(len(near)):
        b2(j).start()

    each(1, 4, lambda o: qd(o).wait_recv())
    lane_part = iota((64, 128), 1) >> 5
    for i in range(ROWS):
        plain = [qd_recv[p, 32 * i:32 * (i + 1), :].astype(F32) for p in range(4)]
        rolled = [jnp.concatenate([one[:, 64:], one[:, :64]], axis=1) for one in plain]
        for a in range(4):
            first = jnp.concatenate([one[8 * a:8 * a + 8] for one in plain], axis=0)
            other = jnp.concatenate([one[8 * a:8 * a + 8] for one in rolled], axis=0)
            straight = jnp.concatenate([first, other], axis=0)
            crossed = jnp.concatenate([other, first], axis=0)
            for part in range(4):
                block = straight if part < 2 else crossed
                lhs[a, i, 64 * part:64 * (part + 1), :] = jnp.where(lane_part == part, block, 0.0).astype(BF16)

    each(1, 16, lambda o: kv(o).wait_recv())
    for g in range(4):
        seen = jnp.zeros((16, 128), F32)
        for u in range(4):
            seen = seen + kv_recv[4 * g + u, 96:112, :].astype(F32)
        pen[:, 128 * g:128 * (g + 1)] = 1e9 * (seen - 1.0)
    for i in range(ROWS):
        block = kv_recv[:, 32 * i:32 * (i + 1), :]
        kv_roll[i] = jnp.concatenate([block[:, :, 64:], block[:, :, :64]], axis=2).reshape(512, 128)

    def class_step(step, delta, waits):
        cls = (kappa + delta) % 4
        for j in waits:
            b2(j).wait_recv()
        b_f32[...] = b_all[cls].astype(F32).reshape(512, 128)
        keep = d_f32.at[0 if step == 0 else 1]

        def row(i, carry):
            left = lhs[cls, i]
            right = kv_recv[:, pl.ds(pl.multiple_of(i * 32, 32), 32), :].reshape(512, 128)
            both = lax.dot_general(left, right, NT, preferred_element_type=F32)
            bias_a = jnp.concatenate([b_f32[pl.ds(m, 64, stride=8), :] for m in range(4)], axis=1)
            bias_b = jnp.concatenate([b_f32[pl.ds(m, 64, stride=8), :] for m in range(4, 8)], axis=1)
            s_a = both[0:64] * SCALE + bias_a + pen[pl.ds(i, 1), :]
            s_b = both[128:192] * SCALE + bias_b + pen[pl.ds(i + 8, 1), :]
            dp_a, dp_b = both[64:128], both[192:256]
            top = jnp.max(jnp.maximum(s_a, s_b), axis=1, keepdims=True)
            e_a, e_b = jnp.exp(s_a - top), jnp.exp(s_b - top)
            inv = 1.0 / jnp.sum(e_a + e_b, axis=1, keepdims=True)
            delta_row = jnp.sum(e_a * dp_a + e_b * dp_b, axis=1, keepdims=True) * inv
            p_a, p_b = e_a * inv, e_b * inv
            g_a, g_b = p_a * (dp_a - delta_row), p_b * (dp_b - delta_row)
            for m in range(8):
                one = (g_a if m < 4 else g_b)[:, 128 * (m % 4):128 * (m % 4 + 1)]
                at = pl.ds(m, 64, stride=8)
                keep[at, :] = jnp.where(i == 0, 0.0, keep[at, :]) + one
            g_a, g_b = g_a.astype(BF16), g_b.astype(BF16)
            stack = jnp.concatenate([g_a, p_a.astype(BF16), g_b, p_b.astype(BF16)], axis=0)
            turned = lax.dot_general(left, stack, TN, preferred_element_type=F32)
            if step == 0:
                dkv_t[i] = turned
            else:
                dkv_t[i] += turned
            dq_buf[cls, i] = dot(g_a, right) + dot(g_b, kv_roll[i])
            return carry

        lax.fori_loop(0, ROWS, row, 0)
        d_send[step] = keep[...].astype(BF16).reshape(2, 16, 16, 128)

    def d2(j):
        dz, dxl = near[j]
        step = {0: 0, 1: 1, -1: 2, 2: 3, -2: 3}[dz]
        src, dst = d_send.at[step, (xl + dxl) % 2], d_recv.at[dxl, step]
        if dz in (2, -2):
            half = pl.ds(0, 8) if dz == 2 else pl.ds(8, 8)
            src, dst = src.at[half], dst.at[half]
        return copy(src, dst, d2_ss.at[j], d2_rs.at[j], (at_z(dz, dxl), c))

    index = {pair: j for j, pair in enumerate(near)}
    plan = [(0, [(0, 1)]), (1, [(-1, 0), (-1, 1)]), (3, [(1, 0), (1, 1)]), (2, [(2, 0), (2, 1), (-2, 0), (-2, 1)])]
    outs = [[(0, 1)], [(1, 0), (1, 1)], [(-1, 0), (-1, 1)], [(2, 0), (2, 1), (-2, 0), (-2, 1)]]
    for step, (delta, waits) in enumerate(plan):
        class_step(step, delta, [index[w] for w in waits])
        for w in outs[step]:
            d2(index[w]).start()

    for i in range(ROWS):
        for b in range(4):
            turned = dkv_t[i, :, 128 * b:128 * (b + 1)].T
            dkv_send[4 * b:4 * b + 4, 32 * i:32 * (i + 1), :] = turned.reshape(4, 32, 128).astype(dkv_send.dtype)

    def dkv(o):
        to = (c + o) % 16
        return copy(dkv_send.at[to], dkv_recv.at[c], dkv_ss.at[o], dkv_rs.at[o], (r, to))

    each(1, 16, lambda o: dkv(o).start())
    dkv_recv[c] = dkv_send[c]

    gather = zero_one(
        ((iota((512, 128), 0) >> 7) * 32 + (iota((512, 128), 0) & 127)) == iota((512, 128), 1)
    )
    gather = jnp.where((iota((512, 128), 0) & 127) < 32, gather, jnp.zeros_like(gather))
    packed = []
    for i in range(ROWS):
        row = jnp.concatenate([(dq_buf[a, i] * SCALE).astype(BF16) for a in range(4)], axis=1)
        packed.append(dot(row, gather))
    for p in range(4):
        pieces = [packed[i][32 * x + 8 * p:32 * x + 8 * p + 8] for i in range(ROWS) for x in range(2)]
        dq_send[p] = jnp.concatenate(pieces, axis=0).astype(BF16)

    def dq(o):
        return copy(dq_send.at[(y + o) % 4], dq_recv.at[y], dq_ss.at[o], dq_rs.at[o], (r, at_y(o)))

    each(1, 4, lambda o: dq(o).start())
    dq_recv[y] = dq_send[y]

    for j in range(len(near)):
        d2(j).wait_recv()
    total = d_f32[0, pl.ds(pl.multiple_of(xl * 256, 256), 256), :]
    for dxl in range(2):
        for slot in range(4):
            if dxl or slot:
                total = total + d_recv[dxl, slot].astype(F32).reshape(256, 128)
    d_sum[...] = total.reshape(16, 16, 128)

    def e(o):
        to_y, to_zq, device = yz(o)
        return copy(d_sum.at[to_y * 4 + to_zq], e_recv.at[y, zq], e_ss.at[o], e_rs.at[o], device)

    each(1, 16, lambda o: e(o).start())
    e_recv[y, zq] = d_sum[y * 4 + zq]

    each(1, 4, lambda o: dq(o).wait_recv())
    back = zero_one(iota((64, 64), 0) == class_place(iota((64, 64), 1)))
    heads = dot(jnp.concatenate([dq_recv[h] for h in range(4)], axis=1), swap[...]).astype(BF16)
    for i in range(ROWS):
        block = jnp.concatenate([heads[16 * i:16 * (i + 1), 128 * a:128 * (a + 1)] for a in range(4)], axis=0)
        dq_ref[i] = dot(back, block).astype(BF16)

    each(1, 16, lambda o: dkv(o).wait_recv())
    k_lanes = ((iota((96, 128), 1) >> 5) & 1) == 0
    sums = []
    for h in range(4):
        one = jnp.zeros((96, 128), F32)
        for x in range(2):
            for core in range(2):
                one = one + dkv_recv[x * 8 + h * 2 + core].astype(F32)
        sums.append(jnp.where(k_lanes, one * SCALE, one).astype(BF16))
    heads = dot(jnp.concatenate(sums, axis=1), swap[...]).astype(BF16)
    for i in range(ROWS):
        for half in range(2):
            part = heads[32 * i:32 * (i + 1), 256 * half:256 * (half + 1)]
            dk_ref[i, 32 * half:32 * (half + 1), :] = part[:, :128]
            dv_ref[i, 32 * half:32 * (half + 1), :] = part[:, 128:]

    each(1, 16, lambda o: e(o).wait_recv())
    total = e_recv[:, 0] + e_recv[:, 1] + e_recv[:, 2] + e_recv[:, 3]
    b_wide[...] = total.reshape(64, 128)
    half_back = jnp.where(iota((256, 256), 0) == half_place(iota((256, 256), 1)), 1.0, 0.0)
    for m in range(4):
        pair = jnp.concatenate([b_wide[pl.ds(half * 4 + m, 8, stride=8), :] for half in range(2)], axis=1)
        turned = jnp.dot(pair, half_back, precision=lax.Precision.HIGHEST, preferred_element_type=F32)
        for h in range(4):
            dbias_ref[h, :, 256 * m:256 * (m + 1)] = turned[2 * h:2 * h + 2]

    each(1, 16, lambda o: b1(o).wait_send())
    each(1, 16, lambda o: kv(o).wait_send())
    each(1, 4, lambda o: qd(o).wait_send())
    for j in range(len(near)):
        b2(j).wait_send()
        d2(j).wait_send()
    each(1, 16, lambda o: dkv(o).wait_send())
    each(1, 4, lambda o: dq(o).wait_send())
    each(1, 16, lambda o: e(o).wait_send())


def on_device(queries, keys, values, pair_mask, tri_bias, grad_out):
    sem = pltpu.SemaphoreType.DMA
    vmem = pl.BlockSpec(memory_space=pltpu.VMEM)
    tile = (16, 128)
    return pl.pallas_call(
        kernel,
        name="attention_backward",
        out_shape=(
            jax.ShapeDtypeStruct(queries.shape, BF16),
            jax.ShapeDtypeStruct(keys.shape, BF16),
            jax.ShapeDtypeStruct(values.shape, BF16),
            jax.ShapeDtypeStruct(tri_bias.shape, F32),
        ),
        in_specs=[vmem] * 6,
        out_specs=[vmem] * 4,
        scratch_shapes=[
            pltpu.VMEM((512, 512), BF16),
            pltpu.VMEM((4, 112, 128), BF16),
            pltpu.VMEM((16, 112, 128), BF16),
            pltpu.VMEM((ROWS, 512, 128), BF16),
            pltpu.VMEM((16, 512), F32),
            pltpu.VMEM((4, 96, 128), BF16),
            pltpu.VMEM((4, 96, 128), BF16),
            pltpu.VMEM((4, ROWS, 256, 128), BF16),
            pltpu.VMEM((64, 128), F32),
            pltpu.VMEM((4,) + tile, BF16),
            pltpu.VMEM((4, 2, 16) + tile, BF16),
            pltpu.VMEM((512, 128), F32),
            pltpu.VMEM((2, 512, 128), F32),
            pltpu.VMEM((4, 2, 16) + tile, BF16),
            pltpu.VMEM((2, 4, 16) + tile, BF16),
            pltpu.VMEM((16,) + tile, F32),
            pltpu.VMEM((4, 4) + tile, F32),
            pltpu.VMEM((ROWS, 128, 512), F32),
            pltpu.VMEM((16, 96, 128), BF16),
            pltpu.VMEM((16, 96, 128), BF16),
            pltpu.VMEM((4, ROWS, 64, 128), F32),
            pltpu.VMEM((4, 48, 128), BF16),
            pltpu.VMEM((4, 48, 128), BF16),
            sem((16,)), sem((16,)), sem((4,)), sem((4,)), sem((16,)), sem((16,)), sem((9,)), sem((9,)),
            sem((9,)), sem((9,)), sem((16,)), sem((16,)), sem((16,)), sem((16,)), sem((4,)), sem((4,)),
        ],
        compiler_params=pltpu.CompilerParams(
            collective_id=0, has_side_effects=True, vmem_limit_bytes=40 * 1024 * 1024
        ),
    )(queries, keys, values, pair_mask, tri_bias, grad_out)


def solution(mesh):
    pair = P("row", "col", None)
    bias = P(None, ("col", "row"), None)
    return jax.shard_map(
        on_device,
        mesh=mesh,
        in_specs=(pair, pair, pair, P("row", "col"), bias, pair),
        out_specs=(pair, pair, pair, bias),
        check_vma=False,
    )
```

time: 752 us -> 67.5 us (0.09)
  the two profiles are of different devices: /device:TPU:24 before, /device:TPU:4 now
where the time goes in v1:
time: 67.5 us; the launch traced here: 67.1 us
  Pallas kernels  59.4 us (88%)
  local copies, waits for them, and re-layouts  7.06 us (10%)
    pallas_call x1, Pallas kernels, on_device(): pl.pallas_call(kernel, name='attention_backward', out_shape=(jax.ShapeDty...  59.4 us
    unnamed x16, local copies, waits for them, and re-layouts  7.06 us

profile of v1, /device:TPU:4, one launch (start us, length us, event | category | flops | bytes accessed | tf_op | source)
XLA Modules:
  0.0 67.1 jit_solution(13530817061925509750)
XLA Ops:
  0.6 0.0 copy-start
  0.6 0.8 %copy-done = bf16[3,64,128]{2,1,0:T(8,128)(2,1)S(1)} copy-done((bf16[3,64,128]{2,1,0:T(8,128)(2,1)S(1)}, bf16[3,64,128]{2,1,0:T(8,128)(2,1)}, u32[]{:S(2)}) %copy-start) | copy-done | bytes 49176
  1.4 0.0 copy-start.1
  1.4 0.8 %copy-done.1 = bf16[3,64,128]{2,1,0:T(8,128)(2,1)S(1)} copy-done((bf16[3,64,128]{2,1,0:T(8,128)(2,1)S(1)}, bf16[3,64,128]{2,1,0:T(8,128)(2,1)}, u32[]{:S(2)}) %copy-start.1) | copy-done | bytes 49176
  2.2 0.0 copy-start.2
  2.2 0.8 %copy-done.2 = bf16[3,64,128]{2,1,0:T(8,128)(2,1)S(1)} copy-done((bf16[3,64,128]{2,1,0:T(8,128)(2,1)S(1)}, bf16[3,64,128]{2,1,0:T(8,128)(2,1)}, u32[]{:S(2)}) %copy-start.2) | copy-done | bytes 49176
  3.0 0.0 copy-start.3
  3.0 0.8 %copy-done.3 = bf16[3,64,128]{2,1,0:T(8,128)(2,1)S(1)} copy-done((bf16[3,64,128]{2,1,0:T(8,128)(2,1)S(1)}, bf16[3,64,128]{2,1,0:T(8,128)(2,1)}, u32[]{:S(2)}) %copy-start.3) | copy-done | bytes 49176
  3.8 0.0 copy-start.4
  3.8 0.7 %copy-done.4 = bf16[4,2,1024]{2,1,0:T(2,128)(2,1)S(1)} copy-done((bf16[4,2,1024]{2,1,0:T(2,128)(2,1)S(1)}, bf16[4,2,1024]{2,1,0:T(2,128)(2,1)}, u32[]{:S(2)}) %copy-start.4) | copy-done | bytes 16408
  4.5 0.0 copy-start.5
  4.5 0.7 %copy-done.5 = s32[3,64]{1,0:T(4,128)S(1)} copy-done((s32[3,64]{1,0:T(4,128)S(1)}, s32[3,64]{1,0:T(4,128)}, u32[]{:S(2)}) %copy-start.5) | copy-done | bytes 792
  5.2 59.4 %attention_backward.1 = (bf16[3,64,128]{2,1,0:T(8,128)(2,1)S(1)}, bf16[3,64,128]{2,1,0:T(8,128)(2,1)S(1)}, bf16[3,64,128]{2,1,0:T(8,128)(2,1)S(1)}, f32[4,2,1024]{2,1,0:T(2,128)S(1)}) custom-call(bf16[3,64,128]{2,1,0:T(8,128)(2,1)S(1)} %copy-done, bf16[3,64,128]{2,1,0:T(8,128)(2,1)S(1)} %copy-done.1, bf16[3,64,128]{2,1,0:T(8,128)(2,1)S(1)} %copy-done.2, ...), custom_call_target="tpu_custom_call" | custom-call | tf_op jit(solution)/shard_map/attention_backward/pallas_call | solution.py:338
  64.6 0.6 copy.14
  65.3 0.6 copy.15
  65.9 0.6 copy.16
  66.5 0.6 copy.17
Async XLA Ops:
  0.6 0.8 %copy-start = (bf16[3,64,128]{2,1,0:T(8,128)(2,1)S(1)}, bf16[3,64,128]{2,1,0:T(8,128)(2,1)}, u32[]{:S(2)}) copy-start(bf16[3,64,128]{2,1,0:T(8,128)(2,1)} %q_ref.1) | copy-start | bytes 147460
  1.4 0.8 %copy-start.1 = (bf16[3,64,128]{2,1,0:T(8,128)(2,1)S(1)}, bf16[3,64,128]{2,1,0:T(8,128)(2,1)}, u32[]{:S(2)}) copy-start(bf16[3,64,128]{2,1,0:T(8,128)(2,1)} %k_ref.1) | copy-start | bytes 147460
  2.2 0.8 %copy-start.2 = (bf16[3,64,128]{2,1,0:T(8,128)(2,1)S(1)}, bf16[3,64,128]{2,1,0:T(8,128)(2,1)}, u32[]{:S(2)}) copy-start(bf16[3,64,128]{2,1,0:T(8,128)(2,1)} %v_ref.1) | copy-start | bytes 147460
  3.0 0.8 %copy-start.3 = (bf16[3,64,128]{2,1,0:T(8,128)(2,1)S(1)}, bf16[3,64,128]{2,1,0:T(8,128)(2,1)}, u32[]{:S(2)}) copy-start(bf16[3,64,128]{2,1,0:T(8,128)(2,1)} %do_ref.1) | copy-start | bytes 147460
  3.8 0.7 %copy-start.4 = (bf16[4,2,1024]{2,1,0:T(2,128)(2,1)S(1)}, bf16[4,2,1024]{2,1,0:T(2,128)(2,1)}, u32[]{:S(2)}) copy-start(bf16[4,2,1024]{2,1,0:T(2,128)(2,1)} %bias_ref.1) | copy-start | bytes 49156
  4.5 0.7 %copy-start.5 = (s32[3,64]{1,0:T(4,128)S(1)}, s32[3,64]{1,0:T(4,128)}, u32[]{:S(2)}) copy-start(s32[3,64]{1,0:T(4,128)} %mask_ref.1) | copy-start | bytes 2308

commit v2 on v1

--- a/solution.py
+++ b/solution.py
@@ -40,11 +40,12 @@
 
 
 def kernel(
-    q_ref, k_ref, v_ref, mask_ref, bias_ref, do_ref,
-    dq_ref, dk_ref, dv_ref, dbias_ref,
+    q_hbm, k_hbm, v_hbm, mask_hbm, bias_hbm, do_hbm,
+    dq_hbm, dk_hbm, dv_hbm, dbias_hbm,
+    dq_ref, dk_ref, dv_ref, dbias_ref, q_ref, k_ref, v_ref, mask_ref, bias_ref, do_ref,
     swap, kv_send, kv_recv, kv_roll, pen, qd_send, qd_recv, lhs, b_wide, b_send, b_all, b_f32,
     d_f32, d_send, d_recv, d_sum, e_recv, dkv_t, dkv_send, dkv_recv, dq_buf, dq_send, dq_recv,
-    kv_ss, kv_rs, qd_ss, qd_rs, b1_ss, b1_rs, b2_ss, b2_rs,
+    in_sem, out_sem, kv_ss, kv_rs, qd_ss, qd_rs, b1_ss, b1_rs, b2_ss, b2_rs,
     d2_ss, d2_rs, e_ss, e_rs, dkv_ss, dkv_rs, dq_ss, dq_rs,
 ):
     r, c = lax.axis_index("row"), lax.axis_index("col")
@@ -74,6 +75,15 @@
 
         lax.fori_loop(low, high, body, 0)
 
+    loads = [
+        pltpu.make_async_copy(src, dst, in_sem.at[j])
+        for j, (src, dst) in enumerate((
+            (bias_hbm, bias_ref), (k_hbm, k_ref), (v_hbm, v_ref), (mask_hbm, mask_ref), (q_hbm, q_ref), (do_hbm, do_ref),
+        ))
+    ]
+    for load in loads:
+        load.start()
+
     near = [(0, 1)] + [(dz, dxl) for dz in (1, -1, 2, -2) for dxl in (0, 1)]
     barrier = pltpu.get_barrier_semaphore()
 
@@ -89,6 +99,7 @@
     for dz, dxl in near:
         greet((at_z(dz, dxl), c))
 
+    loads[0].wait()
     wide = jnp.concatenate([bias_ref[h] for h in range(4)], axis=0)
     half_mat = zero_one(half_place(iota((256, 256), 0)) == iota((256, 256), 1))
     for m in range(4):
@@ -100,6 +111,8 @@
     swap_mat = zero_one(swap_place(iota((512, 512), 0)) == iota((512, 512), 1))
     swap[...] = swap_mat
     spread = swap_mat[:256] + swap_mat[256:]
+    for load in loads[1:]:
+        load.wait()
     low_lanes = iota((32, 128), 1) < 64
     mask_lane = (iota((8, 128), 1) >> 5) == c % 4
     mask = mask_ref[...].astype(F32)
@@ -278,7 +291,7 @@
         for slot in range(4):
             if dxl or slot:
                 total = total + d_recv[dxl, slot].astype(F32).reshape(256, 128)
-    d_sum[...] = total.reshape(16, 16, 128)
+    d_sum[...] = total.reshape(16, 16, 128).astype(BF16)
 
     def e(o):
         to_y, to_zq, device = yz(o)
@@ -293,6 +306,11 @@
     for i in range(ROWS):
         block = jnp.concatenate([heads[16 * i:16 * (i + 1), 128 * a:128 * (a + 1)] for a in range(4)], axis=0)
         dq_ref[i] = dot(back, block).astype(BF16)
+    stores = [
+        pltpu.make_async_copy(src, dst, out_sem.at[j])
+        for j, (src, dst) in enumerate(((dq_ref, dq_hbm), (dk_ref, dk_hbm), (dv_ref, dv_hbm), (dbias_ref, dbias_hbm)))
+    ]
+    stores[0].start()
 
     each(1, 16, lambda o: dkv(o).wait_recv())
     k_lanes = ((iota((96, 128), 1) >> 5) & 1) == 0
@@ -310,8 +328,11 @@
             dk_ref[i, 32 * half:32 * (half + 1), :] = part[:, :128]
             dv_ref[i, 32 * half:32 * (half + 1), :] = part[:, 128:]
 
+    stores[1].start()
+    stores[2].start()
+
     each(1, 16, lambda o: e(o).wait_recv())
-    total = e_recv[:, 0] + e_recv[:, 1] + e_recv[:, 2] + e_recv[:, 3]
+    total = sum(e_recv[:, part].astype(F32) for part in range(4))
     b_wide[...] = total.reshape(64, 128)
     half_back = jnp.where(iota((256, 256), 0) == half_place(iota((256, 256), 1)), 1.0, 0.0)
     for m in range(4):
@@ -319,6 +340,8 @@
         turned = jnp.dot(pair, half_back, precision=lax.Precision.HIGHEST, preferred_element_type=F32)
         for h in range(4):
             dbias_ref[h, :, 256 * m:256 * (m + 1)] = turned[2 * h:2 * h + 2]
+
+    stores[3].start()
 
     each(1, 16, lambda o: b1(o).wait_send())
     each(1, 16, lambda o: kv(o).wait_send())
@@ -329,24 +352,46 @@
     each(1, 16, lambda o: dkv(o).wait_send())
     each(1, 4, lambda o: dq(o).wait_send())
     each(1, 16, lambda o: e(o).wait_send())
+    for one in stores:
+        one.wait()
+
+
+def store(*refs):
+    ins, outs, sems = refs[:4], refs[4:8], refs[8]
+    copies = [pltpu.make_async_copy(src, dst, sems.at[j]) for j, (src, dst) in enumerate(zip(ins, outs))]
+    for one in copies:
+        one.start()
+    for one in copies:
+        one.wait()
 
 
 def on_device(queries, keys, values, pair_mask, tri_bias, grad_out):
     sem = pltpu.SemaphoreType.DMA
-    vmem = pl.BlockSpec(memory_space=pltpu.VMEM)
+    hbm = pl.BlockSpec(memory_space=pltpu.HBM)
     tile = (16, 128)
-    return pl.pallas_call(
+    shapes = (
+        jax.ShapeDtypeStruct(queries.shape, BF16),
+        jax.ShapeDtypeStruct(keys.shape, BF16),
+        jax.ShapeDtypeStruct(values.shape, BF16),
+        jax.ShapeDtypeStruct(tri_bias.shape, F32),
+    )
+    grads = pl.pallas_call(
         kernel,
         name="attention_backward",
-        out_shape=(
-            jax.ShapeDtypeStruct(queries.shape, BF16),
-            jax.ShapeDtypeStruct(keys.shape, BF16),
-            jax.ShapeDtypeStruct(values.shape, BF16),
-            jax.ShapeDtypeStruct(tri_bias.shape, F32),
-        ),
-        in_specs=[vmem] * 6,
-        out_specs=[vmem] * 4,
+        out_shape=shapes,
+        in_specs=[hbm] * 6,
+        out_specs=[hbm] * 4,
         scratch_shapes=[
+            pltpu.VMEM(queries.shape, BF16),
+            pltpu.VMEM(keys.shape, BF16),
+            pltpu.VMEM(values.shape, BF16),
+            pltpu.VMEM(tri_bias.shape, F32),
+            pltpu.VMEM(queries.shape, BF16),
+            pltpu.VMEM(keys.shape, BF16),
+            pltpu.VMEM(values.shape, BF16),
+            pltpu.VMEM(pair_mask.shape, jnp.int32),
+            pltpu.VMEM(tri_bias.shape, BF16),
+            pltpu.VMEM(grad_out.shape, BF16),
             pltpu.VMEM((512, 512), BF16),
             pltpu.VMEM((4, 112, 128), BF16),
             pltpu.VMEM((16, 112, 128), BF16),
@@ -362,21 +407,29 @@
             pltpu.VMEM((2, 512, 128), F32),
             pltpu.VMEM((4, 2, 16) + tile, BF16),
             pltpu.VMEM((2, 4, 16) + tile, BF16),
-            pltpu.VMEM((16,) + tile, F32),
-            pltpu.VMEM((4, 4) + tile, F32),
+            pltpu.VMEM((16,) + tile, BF16),
+            pltpu.VMEM((4, 4) + tile, BF16),
             pltpu.VMEM((ROWS, 128, 512), F32),
             pltpu.VMEM((16, 96, 128), BF16),
             pltpu.VMEM((16, 96, 128), BF16),
             pltpu.VMEM((4, ROWS, 64, 128), F32),
             pltpu.VMEM((4, 48, 128), BF16),
             pltpu.VMEM((4, 48, 128), BF16),
-            sem((16,)), sem((16,)), sem((4,)), sem((4,)), sem((16,)), sem((16,)), sem((9,)), sem((9,)),
+            sem((6,)), sem((4,)), sem((16,)), sem((16,)), sem((4,)), sem((4,)), sem((16,)), sem((16,)), sem((9,)), sem((9,)),
             sem((9,)), sem((9,)), sem((16,)), sem((16,)), sem((16,)), sem((16,)), sem((4,)), sem((4,)),
         ],
         compiler_params=pltpu.CompilerParams(
-            collective_id=0, has_side_effects=True, vmem_limit_bytes=40 * 1024 * 1024
+            collective_id=0, has_side_effects=True, vmem_limit_bytes=60 * 1024 * 1024
         ),
     )(queries, keys, values, pair_mask, tri_bias, grad_out)
+    return pl.pallas_call(
+        store,
+        name="store_gradients",
+        out_shape=shapes,
+        in_specs=[pl.BlockSpec(memory_space=pltpu.VMEM)] * 4,
+        out_specs=[hbm] * 4,
+        scratch_shapes=[sem((4,))],
+    )(*grads)
 
 
 def solution(mesh):

time: 67.5 us -> 59.6 us (0.88)
  the two profiles are of different devices: /device:TPU:4 before, /device:TPU:2 now
where the time goes in v2:
time: 59.6 us; the launch traced here: 59.4 us
  Pallas kernels  58.8 us (99%)
  between operations  0.64 us (1%)
    pallas_call x1, Pallas kernels, on_device(): pl.pallas_call(kernel, name='attention_backward', out_shape=shapes, in_sp...  57.2 us
    pallas_call x1, Pallas kernels, on_device(): pl.pallas_call(store, name='store_gradients', out_shape=shapes, in_specs=...  1.55 us

profile of v2, /device:TPU:2, one launch (start us, length us, event | category | flops | bytes accessed | tf_op | source)
XLA Modules:
  0.0 59.4 jit_solution(16733849712093700205)
XLA Ops:
  0.6 57.2 %attention_backward.1 = (bf16[3,64,128]{2,1,0:T(8,128)(2,1)}, bf16[3,64,128]{2,1,0:T(8,128)(2,1)}, bf16[3,64,128]{2,1,0:T(8,128)(2,1)}, f32[4,2,1024]{2,1,0:T(2,128)}) custom-call(bf16[3,64,128]{2,1,0:T(8,128)(2,1)} %q_hbm.1, bf16[3,64,128]{2,1,0:T(8,128)(2,1)} %k_hbm.1, bf16[3,64,128]{2,1,0:T(8,128)(2,1)} %v_hbm.1, s32[3,64]{1,0:T(4,128)} %mask_hbm.1, ...), custom_call_target="tpu_custom_call" | custom-call | tf_op jit(solution)/shard_map/attention_backward/pallas_call | solution.py:378
  57.9 1.5 %store_gradients.1 = (bf16[3,64,128]{2,1,0:T(8,128)(2,1)}, bf16[3,64,128]{2,1,0:T(8,128)(2,1)}, bf16[3,64,128]{2,1,0:T(8,128)(2,1)}, f32[4,2,1024]{2,1,0:T(2,128)}) custom-call(bf16[3,64,128]{2,1,0:T(8,128)(2,1)} %get-tuple-element.8.refs_0_, bf16[3,64,128]{2,1,0:T(8,128)(2,1)} %get-tuple-element.9.refs_1_, bf16[3,64,128]{2,1,0:T(8,128)(2,1)} %get-tuple-element.10.refs_2_, ...), custom_call_target="tpu_custom_call" | custom-call | tf_op jit(solution)/shard_map/store_gradients/pallas_call | solution.py:425

commit v3 on v2

v3 whole, which is shorter than its diff:
```python
import jax
import jax.numpy as jnp
from jax import lax
from jax.experimental import pallas as pl
from jax.experimental.pallas import tpu as pltpu
from jax.sharding import PartitionSpec as P

MESH = pl.DeviceIdType.MESH
F32, BF16 = jnp.float32, jnp.bfloat16
SCALE = 32 ** -0.5
ROWS = 3
UNROLL = 6
NT = (((1,), (1,)), ((), ()))
TN = (((0,), (0,)), ((), ()))


def iota(shape, dim):
    return lax.broadcasted_iota(jnp.int32, shape, dim)


def dot(a, b):
    return jnp.dot(a, b, preferred_element_type=F32)


def zero_one(hit):
    return jnp.where(hit, 1.0, 0.0).astype(BF16)


def class_place(at):
    return ((at >> 1) & 3) * 16 + (at >> 4) * 4 + ((at >> 3) & 1) * 2 + (at & 1)


def swap_place(at):
    return ((at >> 5) & 3) * 128 + (at >> 7) * 32 + (at & 31)


def kernel(
    q_hbm, k_hbm, v_hbm, mask_hbm, bias_hbm, do_hbm,
    dq_hbm, dk_hbm, dv_hbm, dbias_hbm,
    dq_ref, dk_ref, dv_ref, dbias_ref, q_ref, k_ref, v_ref, mask_ref, bias_ref, do_ref,
    swap, kv_send, kv_recv, kv_roll, pen, qd_send, qd_recv, lhs, b_wide, b_send, b_all, b_f32, bias, d_bias,
    d_f32, d_send, d_recv, d_sum, e_recv, dkv_t, dkv_part, dkv_out, dkv_in, dkv_send, dkv_recv, dq_buf, dq_send, dq_recv,
    hello, in_sem, out_sem, b1_ss, b1_rs, kv_ss, kv_rs, qd_ss, qd_rs, b2_ss, b2_rs, sh_ss, sh_rs,
    d2_ss, d2_rs, x_sem, dq_ss, dq_rs, dkv_ss, dkv_rs, e_ss, e_rs,
):
    r, c = lax.axis_index("row"), lax.axis_index("col")
    z, xl = r // 2, r % 2
    xh, y, core = c // 8, (c // 2) % 4, c % 2
    x = xh * 2 + xl
    zq, kappa = z // 4, z % 4
    sibling = (r, c + 1 - 2 * core)

    def place(at_z, at_x, at_y):
        return (at_z * 2 + at_x % 2, (at_x // 2) * 8 + at_y * 2 + core)

    def yz(o):
        to_y, to_z = (y + o // 4) % 4, (z + (o % 4) * 4) % 16
        return to_y, to_z // 4, place(to_z, x, to_y)

    def yx(o):
        to_y, to_x = (y + o % 4) % 4, (x + o // 4) % 4
        return to_y, to_x, place(z, to_x, to_y)

    def yl(o):
        to_y, to_l = (y + o % 4) % 4, (xl + o // 4) % 2
        return to_y, to_l, place(z, xh * 2 + to_l, to_y)

    def along(dz):
        return place((z + dz + 16) % 16, x, y)

    def copy(src, dst, ss, rs, device):
        return pltpu.make_async_remote_copy(
            src_ref=src, dst_ref=dst, send_sem=ss, recv_sem=rs, device_id=device, device_id_type=MESH
        )

    def each(low, high, do):
        def body(o, carry):
            do(o)
            return carry

        lax.fori_loop(low, high, body, 0)

    loads = [
        pltpu.make_async_copy(src, dst, in_sem.at[j])
        for j, (src, dst) in enumerate((
            (bias_hbm, bias_ref), (k_hbm, k_ref), (v_hbm, v_ref), (mask_hbm, mask_ref), (q_hbm, q_ref), (do_hbm, do_ref),
        ))
    ]
    for load in loads:
        load.start()

    near = (1, -1, 2, -2)
    barrier = pltpu.get_barrier_semaphore()

    def greet(device):
        pl.semaphore_signal(barrier, inc=1, device_id=device, device_id_type=MESH)

    def greet_far(o):
        greet(place((z + (o // 4) * 4) % 16, x, (y + o % 4) % 4))

    each(4, 16, greet_far)
    for dz in near:
        greet(along(dz))
    each(1, 16, lambda o: greet(yx(o)[2]))

    @pl.when(core == 0)
    def _():
        greet(sibling)

    swap_mat = zero_one(swap_place(iota((512, 512), 0)) == iota((512, 512), 1))
    swap[...] = swap_mat
    loads[0].wait()
    wide = jnp.concatenate([bias_ref[h] for h in range(4)], axis=0)
    for at_x in range(2):
        turned = dot(wide[:, 512 * at_x:512 * (at_x + 1)], swap_mat)
        for part in range(4):
            b_wide[pl.ds((part % 2) * 4 + (part // 2) * 2 + at_x, 8, stride=8), :] = turned[:, 128 * part:128 * (part + 1)]
    b_send[...] = b_wide[...].astype(BF16).reshape(4, 16, 128)

    for load in loads[1:]:
        load.wait()
    spread = swap_mat[:256] + swap_mat[256:]
    low_lanes = iota((32, 128), 1) < 64
    mask_lane = (iota((8, 128), 1) >> 5) == y
    mask = mask_ref[...].astype(F32)
    tiles = []
    for half in range(2):
        part = mask[:, 32 * half:32 * (half + 1)]
        part = jnp.concatenate([part] * 4, axis=1)
        part = jnp.concatenate([part, jnp.zeros((8 - ROWS, 128), F32)], axis=0)
        tiles.append(jnp.where(mask_lane, part, 0.0))
    mask_tile = jnp.concatenate(tiles, axis=0).astype(BF16)
    for h in range(4):
        kv_send[h, 96:112, :] = mask_tile
    for i in range(ROWS):
        pairs = dot(jnp.concatenate([k_ref[i], v_ref[i]], axis=1), spread)
        for h in range(4):
            one = pairs[:, 128 * h:128 * (h + 1)]
            kv_send[h, 32 * i:32 * (i + 1), :] = jnp.where(low_lanes, one[:32], one[32:]).astype(BF16)
    order = zero_one(class_place(iota((64, 64), 0)) == iota((64, 64), 1))
    low8 = iota((8, 128), 1) < 64
    for i in range(ROWS):
        turned = dot(order, jnp.concatenate([q_ref[i], do_ref[i]], axis=1)).astype(BF16)
        pairs = dot(turned, spread)
        for h in range(4):
            one = pairs[:, 128 * h:128 * (h + 1)]
            for to_l in range(2):
                eight = [one[16 * a + 8 * to_l:16 * a + 8 * to_l + 8] for a in range(4)]
                parts = [jnp.where(low8, eight[2 * p], eight[2 * p + 1]) for p in range(2)]
                qd_send[to_l, h, 16 * i:16 * (i + 1), :] = jnp.concatenate(parts, axis=0).astype(BF16)

    pl.semaphore_wait(barrier, 12 + 15 + len(near) + core)

    @pl.when(core == 1)
    def _():
        pl.semaphore_signal(hello, inc=1, device_id=sibling, device_id_type=MESH)

    def b1(o):
        to_y, _, device = yz(o)
        return copy(b_send.at[to_y], b_all.at[kappa, y * 4 + zq], b1_ss.at[o], b1_rs.at[o], device)

    def kv(o):
        to_y, _, device = yx(o)
        return copy(kv_send.at[to_y], kv_recv.at[core, xl, xh * 4 + y], kv_ss.at[o], kv_rs.at[o], device)

    def qd(o):
        to_y, to_l, device = yl(o)
        return copy(qd_send.at[to_l, to_y], qd_recv.at[xl, y], qd_ss.at[o], qd_rs.at[o], device)

    each(1, 16, lambda o: b1(o).start())
    each(1, 16, lambda o: kv(o).start())
    each(1, 8, lambda o: qd(o).start())
    b_all[kappa, y * 4 + zq] = b_send[y]
    kv_recv[core, xl, xh * 4 + y] = kv_send[y]
    qd_recv[xl, y] = qd_send[xl, y]

    each(1, 16, lambda o: b1(o).wait_recv())

    def half_of(dz):
        return pl.ds(0, 8) if dz == 2 else pl.ds(8, 8)

    def b2(j):
        dz = near[j]
        mine = b_all.at[kappa]
        if dz in (2, -2):
            mine = mine.at[half_of(dz)]
        return copy(mine, mine, b2_ss.at[j], b2_rs.at[j], along(dz))

    for j in range(len(near)):
        b2(j).start()

    def share(part):
        slab = kv_recv.at[core, (xl + part) % 2]
        return copy(slab, slab, sh_ss.at[part], sh_rs.at[part], sibling)

    each(1, 4, lambda o: kv(o).wait_recv())
    each(8, 12, lambda o: kv(o).wait_recv())

    @pl.when(core == 0)
    def _():
        pl.semaphore_wait(hello, 1)

    share(0).start()
    each(4, 8, lambda o: kv(o).wait_recv())
    each(12, 16, lambda o: kv(o).wait_recv())
    share(1).start()

    each(1, 8, lambda o: qd(o).wait_recv())
    lane_part = iota((32, 128), 1) >> 5
    for row in range(2 * ROWS):
        i = row % ROWS
        plain = [qd_recv[row // ROWS, p, 16 * i:16 * (i + 1), :].astype(F32) for p in range(4)]
        rolled = [jnp.concatenate([one[:, 64:], one[:, :64]], axis=1) for one in plain]
        for a in range(4):
            at = 8 * (a // 2)
            straight = jnp.concatenate([one[at:at + 8] for one in plain], axis=0)
            crossed = jnp.concatenate([one[at:at + 8] for one in rolled], axis=0)
            for part in range(4):
                block = straight if part // 2 == a % 2 else crossed
                at_row = 128 * part + 32 * a
                lhs[row, at_row:at_row + 32, :] = jnp.where(lane_part == part, block, 0.0).astype(BF16)

    for part in range(2):
        share(part).wait_recv()
    for at_l in range(2):
        for g in range(4):
            seen = jnp.zeros((16, 128), F32)
            for u in range(4):
                seen = seen + kv_recv[g // 2, at_l, (g % 2) * 4 + u, 96:112, :].astype(F32)
            pen[at_l, :, 128 * g:128 * (g + 1)] = 1e9 * (seen - 1.0)
        for i in range(ROWS):
            block = kv_recv[:, at_l, :, 32 * i:32 * (i + 1), :]
            kv_roll[at_l * ROWS + i] = jnp.concatenate([block[..., 64:], block[..., :64]], axis=3).reshape(512, 128)

    for j in range(len(near)):
        b2(j).wait_recv()
    b_f32[...] = b_all[...].astype(F32).reshape(1024, 128)
    for m in range(8):
        bias[:, 128 * m:128 * (m + 1)] = b_f32[pl.ds(m, 128, stride=8), :]
    d_bias[...] = jnp.zeros_like(d_bias)

    def attention_row(at, carry):
        at_l, i = at // ROWS, at % ROWS
        left = lhs[at]
        right = kv_recv[:, at_l, :, pl.ds(pl.multiple_of(i * 32, 32), 32), :].reshape(512, 128)
        both = lax.dot_general(left, right, NT, preferred_element_type=F32)
        s_a = both[0:128] * SCALE + bias[:, :512] + pen[at_l, pl.ds(i, 1), :]
        s_b = both[256:384] * SCALE + bias[:, 512:] + pen[at_l, pl.ds(i + 8, 1), :]
        dp_a, dp_b = both[128:256], both[384:512]
        top = jnp.max(jnp.maximum(s_a, s_b), axis=1, keepdims=True)
        e_a, e_b = jnp.exp(s_a - top), jnp.exp(s_b - top)
        inv = 1.0 / jnp.sum(e_a + e_b, axis=1, keepdims=True)
        delta_row = jnp.sum(e_a * dp_a + e_b * dp_b, axis=1, keepdims=True) * inv
        p_a, p_b = e_a * inv, e_b * inv
        g_a, g_b = p_a * (dp_a - delta_row), p_b * (dp_b - delta_row)
        d_bias[:, :512] += g_a
        d_bias[:, 512:] += g_b
        g_a, g_b = g_a.astype(BF16), g_b.astype(BF16)
        stack = jnp.concatenate([g_a, p_a.astype(BF16), g_b, p_b.astype(BF16)], axis=0)
        dkv_t[at] = lax.dot_general(left, stack, TN, preferred_element_type=F32)
        dq_buf[at] = (dot(g_a, right) + dot(g_b, kv_roll[at])) * SCALE
        return carry

    lax.fori_loop(0, 2 * ROWS, attention_row, 0, unroll=UNROLL)
    for m in range(8):
        d_f32[pl.ds(m, 128, stride=8), :] = d_bias[:, 128 * m:128 * (m + 1)]
    d_send[...] = d_f32[...].astype(BF16).reshape(4, 16, 16, 128)

    def d2(j):
        dz = near[j]
        src, dst = d_send.at[(kappa + dz + 4) % 4], d_recv.at[{1: 0, -1: 1, 2: 2, -2: 2}[dz]]
        if dz in (2, -2):
            src, dst = src.at[half_of(dz)], dst.at[half_of(dz)]
        return copy(src, dst, d2_ss.at[j], d2_rs.at[j], along(dz))

    for j in range(len(near)):
        d2(j).start()

    for row in range(2 * ROWS):
        for b in range(4):
            turned = dkv_t[row, :, 128 * b:128 * (b + 1)].T.reshape(4, 32, 128)
            i = row % ROWS
            dkv_part[b // 2, row // ROWS, (b % 2) * 4:(b % 2) * 4 + 4, 32 * i:32 * (i + 1), :] = turned
    dkv_out[...] = dkv_part[1 - core].astype(BF16)
    cross = copy(dkv_out, dkv_in, x_sem.at[0], x_sem.at[1], sibling)
    cross.start()

    gather = zero_one(
        ((iota((512, 128), 0) >> 7) * 32 + (iota((512, 128), 0) & 127)) == iota((512, 128), 1)
    )
    gather = jnp.where((iota((512, 128), 0) & 127) < 32, gather, jnp.zeros_like(gather))
    packed = []
    for row in range(2 * ROWS):
        line = jnp.concatenate([dq_buf[row, 32 * a:32 * (a + 1)].astype(BF16) for a in range(4)], axis=1)
        packed.append(dot(line, gather))
    for to_l in range(2):
        for p in range(4):
            pieces = [packed[to_l * ROWS + i][8 * p:8 * p + 8] for i in range(ROWS)]
            dq_send[to_l, p] = jnp.concatenate(pieces + [jnp.zeros((8, 128), F32)], axis=0).astype(BF16)

    def dq(o):
        to_y, to_l, device = yl(o)
        return copy(dq_send.at[to_l, to_y], dq_recv.at[xl, y], dq_ss.at[o], dq_rs.at[o], device)

    each(1, 8, lambda o: dq(o).start())
    dq_recv[xl, y] = dq_send[xl, y]

    cross.wait_recv()
    dkv_send[...] = (dkv_part[core] + dkv_in[...].astype(F32)).astype(BF16)

    def dkv(o):
        to_y, to_x, device = yx(o)
        src = dkv_send.at[to_x % 2, (to_x // 2) * 4 + to_y]
        return copy(src, dkv_recv.at[x, y], dkv_ss.at[o], dkv_rs.at[o], device)

    each(1, 16, lambda o: dkv(o).start())
    dkv_recv[x, y] = dkv_send[xl, xh * 4 + y]

    for j in range(len(near)):
        d2(j).wait_recv()
    total = d_f32[pl.ds(pl.multiple_of(kappa * 256, 256), 256), :]
    for slot in range(3):
        total = total + d_recv[slot].astype(F32).reshape(256, 128)
    d_sum[...] = total.reshape(16, 16, 128).astype(BF16)

    def e(o):
        to_y, to_zq, device = yz(o)
        return copy(d_sum.at[to_y * 4 + to_zq], e_recv.at[y, zq], e_ss.at[o], e_rs.at[o], device)

    each(1, 16, lambda o: e(o).start())
    e_recv[y, zq] = d_sum[y * 4 + zq]

    each(1, 8, lambda o: dq(o).wait_recv())
    back = zero_one(iota((64, 64), 0) == class_place(iota((64, 64), 1)))
    heads = []
    for h in range(4):
        got = [dq_recv[at_l, h].astype(F32) for at_l in range(2)]
        heads.append(jnp.concatenate([got[at_l][8 * i:8 * i + 8] for i in range(ROWS) for at_l in range(2)], axis=0))
    heads = dot(jnp.concatenate(heads, axis=1).astype(BF16), swap[...]).astype(BF16)
    for i in range(ROWS):
        block = jnp.concatenate([heads[16 * i:16 * (i + 1), 128 * a:128 * (a + 1)] for a in range(4)], axis=0)
        dq_ref[i] = dot(back, block).astype(BF16)
    stores = [
        pltpu.make_async_copy(src, dst, out_sem.at[j])
        for j, (src, dst) in enumerate(((dq_ref, dq_hbm), (dk_ref, dk_hbm), (dv_ref, dv_hbm), (dbias_ref, dbias_hbm)))
    ]
    stores[0].start()

    each(1, 16, lambda o: dkv(o).wait_recv())
    k_lanes = ((iota((96, 128), 1) >> 5) & 1) == 0
    sums = []
    for h in range(4):
        one = sum(dkv_recv[at_x, h].astype(F32) for at_x in range(4))
        sums.append(jnp.where(k_lanes, one * SCALE, one).astype(BF16))
    heads = dot(jnp.concatenate(sums, axis=1), swap[...]).astype(BF16)
    for i in range(ROWS):
        for half in range(2):
            part = heads[32 * i:32 * (i + 1), 256 * half:256 * (half + 1)]
            dk_ref[i, 32 * half:32 * (half + 1), :] = part[:, :128]
            dv_ref[i, 32 * half:32 * (half + 1), :] = part[:, 128:]
    stores[1].start()
    stores[2].start()

    each(1, 16, lambda o: e(o).wait_recv())
    b_wide[...] = sum(e_recv[:, part].astype(F32) for part in range(4)).reshape(64, 128)
    for at_x in range(2):
        lines = [b_wide[pl.ds((part % 2) * 4 + (part // 2) * 2 + at_x, 8, stride=8), :] for part in range(4)]
        rest = jnp.concatenate(lines, axis=1)
        terms = []
        for _ in range(3):
            terms.append(rest.astype(BF16).astype(F32))
            rest = rest - terms[-1]
        turned = dot(jnp.concatenate(terms, axis=0).astype(BF16), swap[...])
        turned = turned[:8] + turned[8:16] + turned[16:]
        for h in range(4):
            dbias_ref[h, :, 512 * at_x:512 * (at_x + 1)] = turned[2 * h:2 * h + 2]
    stores[3].start()

    each(1, 16, lambda o: b1(o).wait_send())
    each(1, 16, lambda o: kv(o).wait_send())
    each(1, 8, lambda o: qd(o).wait_send())
    for j in range(len(near)):
        b2(j).wait_send()
        d2(j).wait_send()
    for part in range(2):
        share(part).wait_send()
    cross.wait_send()
    each(1, 16, lambda o: dkv(o).wait_send())
    each(1, 8, lambda o: dq(o).wait_send())
    each(1, 16, lambda o: e(o).wait_send())
    for one in stores:
        one.wait()


def store(*refs):
    ins, outs, sems = refs[:4], refs[4:8], refs[8]
    copies = [pltpu.make_async_copy(src, dst, sems.at[j]) for j, (src, dst) in enumerate(zip(ins, outs))]
    for one in copies:
        one.start()
    for one in copies:
        one.wait()


def on_device(queries, keys, values, pair_mask, tri_bias, grad_out):
    sem = pltpu.SemaphoreType.DMA
    hbm = pl.BlockSpec(memory_space=pltpu.HBM)
    tile = (16, 128)
    shapes = (
        jax.ShapeDtypeStruct(queries.shape, BF16),
        jax.ShapeDtypeStruct(keys.shape, BF16),
        jax.ShapeDtypeStruct(values.shape, BF16),
        jax.ShapeDtypeStruct(tri_bias.shape, F32),
    )
    grads = pl.pallas_call(
        kernel,
        name="attention_backward",
        out_shape=shapes,
        in_specs=[hbm] * 6,
        out_specs=[hbm] * 4,
        scratch_shapes=[
            pltpu.VMEM(queries.shape, BF16),
            pltpu.VMEM(keys.shape, BF16),
            pltpu.VMEM(values.shape, BF16),
            pltpu.VMEM(tri_bias.shape, F32),
            pltpu.VMEM(queries.shape, BF16),
            pltpu.VMEM(keys.shape, BF16),
            pltpu.VMEM(values.shape, BF16),
            pltpu.VMEM(pair_mask.shape, jnp.int32),
            pltpu.VMEM(tri_bias.shape, BF16),
            pltpu.VMEM(grad_out.shape, BF16),
            pltpu.VMEM((512, 512), BF16),
            pltpu.VMEM((4, 112, 128), BF16),
            pltpu.VMEM((2, 2, 8, 112, 128), BF16),
            pltpu.VMEM((2 * ROWS, 512, 128), BF16),
            pltpu.VMEM((2, 16, 512), F32),
            pltpu.VMEM((2, 4, 48, 128), BF16),
            pltpu.VMEM((2, 4, 48, 128), BF16),
            pltpu.VMEM((2 * ROWS, 512, 128), BF16),
            pltpu.VMEM((64, 128), F32),
            pltpu.VMEM((4,) + tile, BF16),
            pltpu.VMEM((4, 16) + tile, BF16),
            pltpu.VMEM((1024, 128), F32),
            pltpu.VMEM((128, 1024), F32),
            pltpu.VMEM((128, 1024), F32),
            pltpu.VMEM((1024, 128), F32),
            pltpu.VMEM((4, 16) + tile, BF16),
            pltpu.VMEM((3, 16) + tile, BF16),
            pltpu.VMEM((16,) + tile, BF16),
            pltpu.VMEM((4, 4) + tile, BF16),
            pltpu.VMEM((2 * ROWS, 128, 512), F32),
            pltpu.VMEM((2, 2, 8, 96, 128), F32),
            pltpu.VMEM((2, 8, 96, 128), BF16),
            pltpu.VMEM((2, 8, 96, 128), BF16),
            pltpu.VMEM((2, 8, 96, 128), BF16),
            pltpu.VMEM((4, 4, 96, 128), BF16),
            pltpu.VMEM((2 * ROWS, 128, 128), F32),
            pltpu.VMEM((2, 4, 32, 128), BF16),
            pltpu.VMEM((2, 4, 32, 128), BF16),
            pltpu.SemaphoreType.REGULAR, sem((6,)), sem((4,)),
            sem((16,)), sem((16,)), sem((16,)), sem((16,)), sem((8,)), sem((8,)), sem((4,)), sem((4,)), sem((2,)), sem((2,)),
            sem((4,)), sem((4,)), sem((2,)), sem((8,)), sem((8,)), sem((16,)), sem((16,)), sem((16,)), sem((16,)),
        ],
        compiler_params=pltpu.CompilerParams(
            collective_id=0, has_side_effects=True, vmem_limit_bytes=60 * 1024 * 1024
        ),
    )(queries, keys, values, pair_mask, tri_bias, grad_out)
    return pl.pallas_call(
        store,
        name="store_gradients",
        out_shape=shapes,
        in_specs=[pl.BlockSpec(memory_space=pltpu.VMEM)] * 4,
        out_specs=[hbm] * 4,
        scratch_shapes=[sem((4,))],
    )(*grads)


def solution(mesh):
    pair = P("row", "col", None)
    bias = P(None, ("col", "row"), None)
    return jax.shard_map(
        on_device,
        mesh=mesh,
        in_specs=(pair, pair, pair, P("row", "col"), bias, pair),
        out_specs=(pair, pair, pair, bias),
        check_vma=False,
    )
```

time: 59.6 us -> 54 us (0.906)
  the two profiles are of different devices: /device:TPU:2 before, /device:TPU:64 now
where the time goes in v3:
time: 54 us; the launch traced here: 53.8 us
  Pallas kernels  53.2 us (99%)
  between operations  0.64 us (1%)
    pallas_call x1, Pallas kernels, on_device(): pl.pallas_call(kernel, name='attention_backward', out_shape=shapes, in_sp...  51.6 us
    pallas_call x1, Pallas kernels, on_device(): pl.pallas_call(store, name='store_gradients', out_shape=shapes, in_specs=...  1.55 us

profile of v3, /device:TPU:64, one launch (start us, length us, event | category | flops | bytes accessed | tf_op | source)
XLA Modules:
  0.0 53.8 jit_solution(1412721822357230994)
XLA Ops:
  0.6 51.6 %attention_backward.1 = (bf16[3,64,128]{2,1,0:T(8,128)(2,1)}, bf16[3,64,128]{2,1,0:T(8,128)(2,1)}, bf16[3,64,128]{2,1,0:T(8,128)(2,1)}, f32[4,2,1024]{2,1,0:T(2,128)}) custom-call(bf16[3,64,128]{2,1,0:T(8,128)(2,1)} %q_hbm.1, bf16[3,64,128]{2,1,0:T(8,128)(2,1)} %k_hbm.1, bf16[3,64,128]{2,1,0:T(8,128)(2,1)} %v_hbm.1, s32[3,64]{1,0:T(4,128)} %mask_hbm.1, ...), custom_call_target="tpu_custom_call" | custom-call | tf_op jit(solution)/shard_map/attention_backward/pallas_call | solution.py:414
  52.3 1.5 %store_gradients.1 = (bf16[3,64,128]{2,1,0:T(8,128)(2,1)}, bf16[3,64,128]{2,1,0:T(8,128)(2,1)}, bf16[3,64,128]{2,1,0:T(8,128)(2,1)}, f32[4,2,1024]{2,1,0:T(2,128)}) custom-call(bf16[3,64,128]{2,1,0:T(8,128)(2,1)} %get-tuple-element.8.refs_0_, bf16[3,64,128]{2,1,0:T(8,128)(2,1)} %get-tuple-element.9.refs_1_, bf16[3,64,128]{2,1,0:T(8,128)(2,1)} %get-tuple-element.10.refs_2_, ...), custom_call_target="tpu_custom_call" | custom-call | tf_op jit(solution)/shard_map/store_gradients/pallas_call | solution.py:467

commit v4 on v3

--- a/solution.py
+++ b/solution.py
@@ -26,8 +26,12 @@
     return jnp.where(hit, 1.0, 0.0).astype(BF16)
 
 
-def class_place(at):
-    return ((at >> 1) & 3) * 16 + (at >> 4) * 4 + ((at >> 3) & 1) * 2 + (at & 1)
+def query_place(at):
+    return ((at >> 1) & 15) * 4 + (at >> 5) * 2 + (at & 1)
+
+
+def grad_place(at):
+    return (at >> 4) * 16 + ((at >> 1) & 3) * 4 + ((at >> 3) & 1) * 2 + (at & 1)
 
 
 def swap_place(at):
@@ -38,24 +42,22 @@
     q_hbm, k_hbm, v_hbm, mask_hbm, bias_hbm, do_hbm,
     dq_hbm, dk_hbm, dv_hbm, dbias_hbm,
     dq_ref, dk_ref, dv_ref, dbias_ref, q_ref, k_ref, v_ref, mask_ref, bias_ref, do_ref,
-    swap, kv_send, kv_recv, kv_roll, pen, qd_send, qd_recv, lhs, b_wide, b_send, b_all, b_f32, bias, d_bias,
-    d_f32, d_send, d_recv, d_sum, e_recv, dkv_t, dkv_part, dkv_out, dkv_in, dkv_send, dkv_recv, dq_buf, dq_send, dq_recv,
-    hello, in_sem, out_sem, b1_ss, b1_rs, kv_ss, kv_rs, qd_ss, qd_rs, b2_ss, b2_rs, sh_ss, sh_rs,
-    d2_ss, d2_rs, x_sem, dq_ss, dq_rs, dkv_ss, dkv_rs, e_ss, e_rs,
+    swap, kv_send, kv_recv, pen, qd_send, qd_recv, lhs, b_wide, b_send, b_all, b_f32, bias, d_bias,
+    d_f32, d_send, d_recv, d_half, d_sum, e_recv, dkv_t, dkv_part, dkv_out, dkv_in, dkv_send, dkv_recv, dq_buf, dq_send, dq_recv,
+    hello, in_sem, out_sem, b1_sem, kv_ss, kv_rs, qd_sem, b2_sem, sh_ss, sh_rs, d2_sem, x_sem, dq_sem, dkv_sem, e_sem,
 ):
     r, c = lax.axis_index("row"), lax.axis_index("col")
     z, xl = r // 2, r % 2
     xh, y, core = c // 8, (c // 2) % 4, c % 2
     x = xh * 2 + xl
-    zq, kappa = z // 4, z % 4
     sibling = (r, c + 1 - 2 * core)
 
     def place(at_z, at_x, at_y):
         return (at_z * 2 + at_x % 2, (at_x // 2) * 8 + at_y * 2 + core)
 
     def yz(o):
-        to_y, to_z = (y + o // 4) % 4, (z + (o % 4) * 4) % 16
-        return to_y, to_z // 4, place(to_z, x, to_y)
+        to_y, step = (y + o % 4) % 4, o // 4
+        return to_y, step, place((z + 5 * step + step // 2) % 16, x, to_y)
 
     def yx(o):
         to_y, to_x = (y + o % 4) % 4, (x + o // 4) % 4
@@ -79,6 +81,16 @@
             return carry
 
         lax.fori_loop(low, high, body, 0)
+
+    def arrived(ref, sem):
+        pltpu.make_async_remote_copy(
+            src_ref=ref, dst_ref=ref, send_sem=sem, recv_sem=sem, device_id=sibling, device_id_type=MESH
+        ).wait_recv()
+
+    def left(ref, sem):
+        pltpu.make_async_remote_copy(
+            src_ref=ref, dst_ref=ref, send_sem=sem, recv_sem=sem, device_id=sibling, device_id_type=MESH
+        ).wait_send()
 
     loads = [
         pltpu.make_async_copy(src, dst, in_sem.at[j])
@@ -89,16 +101,14 @@
     for load in loads:
         load.start()
 
-    near = (1, -1, 2, -2)
+    near = (1, -1, 2, -2, 3, -3)
+    hops = (0, 5, -5)
     barrier = pltpu.get_barrier_semaphore()
 
     def greet(device):
         pl.semaphore_signal(barrier, inc=1, device_id=device, device_id_type=MESH)
 
-    def greet_far(o):
-        greet(place((z + (o // 4) * 4) % 16, x, (y + o % 4) % 4))
-
-    each(4, 16, greet_far)
+    each(4, 12, lambda o: greet(yz(o)[2]))
     for dz in near:
         greet(along(dz))
     each(1, 16, lambda o: greet(yx(o)[2]))
@@ -137,19 +147,18 @@
         for h in range(4):
             one = pairs[:, 128 * h:128 * (h + 1)]
             kv_send[h, 32 * i:32 * (i + 1), :] = jnp.where(low_lanes, one[:32], one[32:]).astype(BF16)
-    order = zero_one(class_place(iota((64, 64), 0)) == iota((64, 64), 1))
-    low8 = iota((8, 128), 1) < 64
+    order = zero_one(query_place(iota((64, 64), 0)) == iota((64, 64), 1))
+    low16 = iota((16, 128), 1) < 64
     for i in range(ROWS):
         turned = dot(order, jnp.concatenate([q_ref[i], do_ref[i]], axis=1)).astype(BF16)
         pairs = dot(turned, spread)
         for h in range(4):
             one = pairs[:, 128 * h:128 * (h + 1)]
             for to_l in range(2):
-                eight = [one[16 * a + 8 * to_l:16 * a + 8 * to_l + 8] for a in range(4)]
-                parts = [jnp.where(low8, eight[2 * p], eight[2 * p + 1]) for p in range(2)]
-                qd_send[to_l, h, 16 * i:16 * (i + 1), :] = jnp.concatenate(parts, axis=0).astype(BF16)
-
-    pl.semaphore_wait(barrier, 12 + 15 + len(near) + core)
+                pair = jnp.where(low16, one[32 * to_l:32 * to_l + 16], one[32 * to_l + 16:32 * to_l + 32])
+                qd_send[to_l, h, 16 * i:16 * (i + 1), :] = pair.astype(BF16)
+
+    pl.semaphore_wait(barrier, 8 + 15 + len(near) + core)
 
     @pl.when(core == 1)
     def _():
@@ -157,68 +166,65 @@
 
     def b1(o):
         to_y, _, device = yz(o)
-        return copy(b_send.at[to_y], b_all.at[kappa, y * 4 + zq], b1_ss.at[o], b1_rs.at[o], device)
+        return copy(b_send.at[to_y], b_all.at[y, z], b1_sem.at[0], b1_sem.at[1], device)
 
     def kv(o):
         to_y, _, device = yx(o)
-        return copy(kv_send.at[to_y], kv_recv.at[core, xl, xh * 4 + y], kv_ss.at[o], kv_rs.at[o], device)
+        return copy(kv_send.at[to_y], kv_recv.at[core, xl, xh * 4 + y], kv_ss.at[(o // 4) % 2], kv_rs.at[(o // 4) % 2], device)
 
     def qd(o):
         to_y, to_l, device = yl(o)
-        return copy(qd_send.at[to_l, to_y], qd_recv.at[xl, y], qd_ss.at[o], qd_rs.at[o], device)
-
-    each(1, 16, lambda o: b1(o).start())
+        return copy(qd_send.at[to_l, to_y], qd_recv.at[xl * 4 + y], qd_sem.at[0], qd_sem.at[1], device)
+
+    each(1, 12, lambda o: b1(o).start())
     each(1, 16, lambda o: kv(o).start())
     each(1, 8, lambda o: qd(o).start())
-    b_all[kappa, y * 4 + zq] = b_send[y]
+    b_all[y, z] = b_send[y]
     kv_recv[core, xl, xh * 4 + y] = kv_send[y]
-    qd_recv[xl, y] = qd_send[xl, y]
-
-    each(1, 16, lambda o: b1(o).wait_recv())
-
-    def half_of(dz):
-        return pl.ds(0, 8) if dz == 2 else pl.ds(8, 8)
-
-    def b2(j):
-        dz = near[j]
-        mine = b_all.at[kappa]
-        if dz in (2, -2):
-            mine = mine.at[half_of(dz)]
-        return copy(mine, mine, b2_ss.at[j], b2_rs.at[j], along(dz))
-
-    for j in range(len(near)):
-        b2(j).start()
+    qd_recv[xl * 4 + y] = qd_send[xl, y]
+
+    arrived(b_all.at[0, pl.ds(0, 11)], b1_sem.at[1])
+
+    def block_of(ref, dz, at_z):
+        part = {3: pl.ds(0, 2), -3: pl.ds(2, 2)}.get(dz, slice(None))
+        return ref.at[part, (at_z + 32) % 16]
+
+    def b2(dz, hop):
+        mine = block_of(b_all, dz, z + hop)
+        return copy(mine, mine, b2_sem.at[0], b2_sem.at[1], along(dz))
+
+    for hop in hops:
+        for dz in near[:4]:
+            b2(dz, hop).start()
+    b2(3, -5).start()
+    b2(-3, 5).start()
 
     def share(part):
         slab = kv_recv.at[core, (xl + part) % 2]
         return copy(slab, slab, sh_ss.at[part], sh_rs.at[part], sibling)
 
-    each(1, 4, lambda o: kv(o).wait_recv())
-    each(8, 12, lambda o: kv(o).wait_recv())
+    arrived(kv_recv.at[core, xl, pl.ds(0, 7)], kv_rs.at[0])
 
     @pl.when(core == 0)
     def _():
         pl.semaphore_wait(hello, 1)
 
     share(0).start()
-    each(4, 8, lambda o: kv(o).wait_recv())
-    each(12, 16, lambda o: kv(o).wait_recv())
+    arrived(kv_recv.at[core, 1 - xl], kv_rs.at[1])
     share(1).start()
 
-    each(1, 8, lambda o: qd(o).wait_recv())
-    lane_part = iota((32, 128), 1) >> 5
+    arrived(qd_recv.at[pl.ds(0, 7)], qd_sem.at[1])
+    lane_part = iota((16, 128), 1) >> 5
     for row in range(2 * ROWS):
         i = row % ROWS
-        plain = [qd_recv[row // ROWS, p, 16 * i:16 * (i + 1), :].astype(F32) for p in range(4)]
-        rolled = [jnp.concatenate([one[:, 64:], one[:, :64]], axis=1) for one in plain]
-        for a in range(4):
-            at = 8 * (a // 2)
-            straight = jnp.concatenate([one[at:at + 8] for one in plain], axis=0)
-            crossed = jnp.concatenate([one[at:at + 8] for one in rolled], axis=0)
-            for part in range(4):
-                block = straight if part // 2 == a % 2 else crossed
-                at_row = 128 * part + 32 * a
-                lhs[row, at_row:at_row + 32, :] = jnp.where(lane_part == part, block, 0.0).astype(BF16)
+        for p in range(4):
+            plain = qd_recv[row // ROWS * 4 + p, 16 * i:16 * (i + 1), :].astype(F32)
+            rolled = pltpu.roll(plain, 64, 1)
+            for half in range(2):
+                for part in range(4):
+                    at_row = 128 * part + 32 * p + 16 * half
+                    block = plain if part // 2 == half else rolled
+                    lhs[row, at_row:at_row + 16, :] = jnp.where(lane_part == part, block, 0.0).astype(BF16)
 
     for part in range(2):
         share(part).wait_recv()
@@ -228,12 +234,8 @@
             for u in range(4):
                 seen = seen + kv_recv[g // 2, at_l, (g % 2) * 4 + u, 96:112, :].astype(F32)
             pen[at_l, :, 128 * g:128 * (g + 1)] = 1e9 * (seen - 1.0)
-        for i in range(ROWS):
-            block = kv_recv[:, at_l, :, 32 * i:32 * (i + 1), :]
-            kv_roll[at_l * ROWS + i] = jnp.concatenate([block[..., 64:], block[..., :64]], axis=3).reshape(512, 128)
-
-    for j in range(len(near)):
-        b2(j).wait_recv()
+
+    arrived(b_all.at[:, pl.ds(0, 13)], b2_sem.at[1])
     b_f32[...] = b_all[...].astype(F32).reshape(1024, 128)
     for m in range(8):
         bias[:, 128 * m:128 * (m + 1)] = b_f32[pl.ds(m, 128, stride=8), :]
@@ -258,7 +260,7 @@
         g_a, g_b = g_a.astype(BF16), g_b.astype(BF16)
         stack = jnp.concatenate([g_a, p_a.astype(BF16), g_b, p_b.astype(BF16)], axis=0)
         dkv_t[at] = lax.dot_general(left, stack, TN, preferred_element_type=F32)
-        dq_buf[at] = (dot(g_a, right) + dot(g_b, kv_roll[at])) * SCALE
+        dq_buf[at] = (dot(g_a, right) + pltpu.roll(dot(g_b, right), 64, 1)) * SCALE
         return carry
 
     lax.fori_loop(0, 2 * ROWS, attention_row, 0, unroll=UNROLL)
@@ -266,15 +268,16 @@
         d_f32[pl.ds(m, 128, stride=8), :] = d_bias[:, 128 * m:128 * (m + 1)]
     d_send[...] = d_f32[...].astype(BF16).reshape(4, 16, 16, 128)
 
-    def d2(j):
-        dz = near[j]
-        src, dst = d_send.at[(kappa + dz + 4) % 4], d_recv.at[{1: 0, -1: 1, 2: 2, -2: 2}[dz]]
-        if dz in (2, -2):
-            src, dst = src.at[half_of(dz)], dst.at[half_of(dz)]
-        return copy(src, dst, d2_ss.at[j], d2_rs.at[j], along(dz))
-
-    for j in range(len(near)):
-        d2(j).start()
+    def d2(dz, hop):
+        src = block_of(d_send, {3: -3, -3: 3}.get(dz, dz), z + dz + hop)
+        dst = d_recv.at[near.index(dz), hops.index(hop)] if dz in near[:4] else d_half.at[hops.index(hop) - 1]
+        return copy(src, dst, d2_sem.at[0], d2_sem.at[1], along(dz))
+
+    for hop in hops[::-1]:
+        for dz in near[:4]:
+            d2(dz, hop).start()
+    d2(3, 5).start()
+    d2(-3, -5).start()
 
     for row in range(2 * ROWS):
         for b in range(4):
@@ -291,7 +294,8 @@
     gather = jnp.where((iota((512, 128), 0) & 127) < 32, gather, jnp.zeros_like(gather))
     packed = []
     for row in range(2 * ROWS):
-        line = jnp.concatenate([dq_buf[row, 32 * a:32 * (a + 1)].astype(BF16) for a in range(4)], axis=1)
+        groups = [jnp.concatenate([dq_buf[row, at:at + 8] for at in range(8 * g, 128, 32)], axis=0) for g in range(4)]
+        line = jnp.concatenate(groups, axis=1).astype(BF16)
         packed.append(dot(line, gather))
     for to_l in range(2):
         for p in range(4):
@@ -300,10 +304,10 @@
 
     def dq(o):
         to_y, to_l, device = yl(o)
-        return copy(dq_send.at[to_l, to_y], dq_recv.at[xl, y], dq_ss.at[o], dq_rs.at[o], device)
+        return copy(dq_send.at[to_l, to_y], dq_recv.at[xl * 4 + y], dq_sem.at[0], dq_sem.at[1], device)
 
     each(1, 8, lambda o: dq(o).start())
-    dq_recv[xl, y] = dq_send[xl, y]
+    dq_recv[xl * 4 + y] = dq_send[xl, y]
 
     cross.wait_recv()
     dkv_send[...] = (dkv_part[core] + dkv_in[...].astype(F32)).astype(BF16)
@@ -311,30 +315,34 @@
     def dkv(o):
         to_y, to_x, device = yx(o)
         src = dkv_send.at[to_x % 2, (to_x // 2) * 4 + to_y]
-        return copy(src, dkv_recv.at[x, y], dkv_ss.at[o], dkv_rs.at[o], device)
+        return copy(src, dkv_recv.at[x * 4 + y], dkv_sem.at[0], dkv_sem.at[1], device)
 
     each(1, 16, lambda o: dkv(o).start())
-    dkv_recv[x, y] = dkv_send[xl, xh * 4 + y]
-
-    for j in range(len(near)):
-        d2(j).wait_recv()
-    total = d_f32[pl.ds(pl.multiple_of(kappa * 256, 256), 256), :]
-    for slot in range(3):
-        total = total + d_recv[slot].astype(F32).reshape(256, 128)
-    d_sum[...] = total.reshape(16, 16, 128).astype(BF16)
+    dkv_recv[x * 4 + y] = dkv_send[xl, xh * 4 + y]
+
+    arrived(d_send.at[:, pl.ds(0, 13)], d2_sem.at[1])
+    for step, hop in enumerate(hops):
+        at_z = (z + hop + 16) % 16
+        for p in range(4):
+            total = d_f32[pl.ds(pl.multiple_of(256 * p + 16 * at_z, 16), 16), :]
+            for slot in range(4):
+                total = total + d_recv[slot, step, p].astype(F32)
+            if step and p // 2 == 2 - step:
+                total = total + d_half[step - 1, p % 2].astype(F32)
+            d_sum[step, p] = total.astype(BF16)
 
     def e(o):
-        to_y, to_zq, device = yz(o)
-        return copy(d_sum.at[to_y * 4 + to_zq], e_recv.at[y, zq], e_ss.at[o], e_rs.at[o], device)
-
-    each(1, 16, lambda o: e(o).start())
-    e_recv[y, zq] = d_sum[y * 4 + zq]
-
-    each(1, 8, lambda o: dq(o).wait_recv())
-    back = zero_one(iota((64, 64), 0) == class_place(iota((64, 64), 1)))
+        to_y, step, device = yz(o)
+        return copy(d_sum.at[step, to_y], e_recv.at[y * 3 + step], e_sem.at[0], e_sem.at[1], device)
+
+    each(1, 12, lambda o: e(o).start())
+    e_recv[y * 3] = d_sum[0, y]
+
+    arrived(dq_recv.at[pl.ds(0, 7)], dq_sem.at[1])
+    back = zero_one(iota((64, 64), 0) == grad_place(iota((64, 64), 1)))
     heads = []
     for h in range(4):
-        got = [dq_recv[at_l, h].astype(F32) for at_l in range(2)]
+        got = [dq_recv[at_l * 4 + h].astype(F32) for at_l in range(2)]
         heads.append(jnp.concatenate([got[at_l][8 * i:8 * i + 8] for i in range(ROWS) for at_l in range(2)], axis=0))
     heads = dot(jnp.concatenate(heads, axis=1).astype(BF16), swap[...]).astype(BF16)
     for i in range(ROWS):
@@ -346,11 +354,11 @@
     ]
     stores[0].start()
 
-    each(1, 16, lambda o: dkv(o).wait_recv())
+    arrived(dkv_recv.at[pl.ds(0, 15)], dkv_sem.at[1])
     k_lanes = ((iota((96, 128), 1) >> 5) & 1) == 0
     sums = []
     for h in range(4):
-        one = sum(dkv_recv[at_x, h].astype(F32) for at_x in range(4))
+        one = sum(dkv_recv[at_x * 4 + h].astype(F32) for at_x in range(4))
         sums.append(jnp.where(k_lanes, one * SCALE, one).astype(BF16))
     heads = dot(jnp.concatenate(sums, axis=1), swap[...]).astype(BF16)
     for i in range(ROWS):
@@ -361,8 +369,21 @@
     stores[1].start()
     stores[2].start()
 
-    each(1, 16, lambda o: e(o).wait_recv())
-    b_wide[...] = sum(e_recv[:, part].astype(F32) for part in range(4)).reshape(64, 128)
+    left(b_all.at[0, pl.ds(0, 11)], b1_sem.at[0])
+    left(kv_recv.at[core, xl, pl.ds(0, 7)], kv_ss.at[0])
+    left(kv_recv.at[core, 1 - xl], kv_ss.at[1])
+    left(qd_recv.at[pl.ds(0, 7)], qd_sem.at[0])
+    left(b_all.at[:, pl.ds(0, 13)], b2_sem.at[0])
+    left(d_send.at[:, pl.ds(0, 13)], d2_sem.at[0])
+    for part in range(2):
+        share(part).wait_send()
+    cross.wait_send()
+    left(dq_recv.at[pl.ds(0, 7)], dq_sem.at[0])
+    left(dkv_recv.at[pl.ds(0, 15)], dkv_sem.at[0])
+    left(e_recv.at[pl.ds(0, 11)], e_sem.at[0])
+    arrived(e_recv.at[pl.ds(0, 11)], e_sem.at[1])
+    for h in range(4):
+        b_wide[16 * h:16 * (h + 1), :] = sum(e_recv[3 * h + step].astype(F32) for step in range(3))
     for at_x in range(2):
         lines = [b_wide[pl.ds((part % 2) * 4 + (part // 2) * 2 + at_x, 8, stride=8), :] for part in range(4)]
         rest = jnp.concatenate(lines, axis=1)
@@ -376,18 +397,6 @@
             dbias_ref[h, :, 512 * at_x:512 * (at_x + 1)] = turned[2 * h:2 * h + 2]
     stores[3].start()
 
-    each(1, 16, lambda o: b1(o).wait_send())
-    each(1, 16, lambda o: kv(o).wait_send())
-    each(1, 8, lambda o: qd(o).wait_send())
-    for j in range(len(near)):
-        b2(j).wait_send()
-        d2(j).wait_send()
-    for part in range(2):
-        share(part).wait_send()
-    cross.wait_send()
-    each(1, 16, lambda o: dkv(o).wait_send())
-    each(1, 8, lambda o: dq(o).wait_send())
-    each(1, 16, lambda o: e(o).wait_send())
     for one in stores:
         one.wait()
 
@@ -431,10 +440,9 @@
             pltpu.VMEM((512, 512), BF16),
             pltpu.VMEM((4, 112, 128), BF16),
             pltpu.VMEM((2, 2, 8, 112, 128), BF16),
-            pltpu.VMEM((2 * ROWS, 512, 128), BF16),
             pltpu.VMEM((2, 16, 512), F32),
             pltpu.VMEM((2, 4, 48, 128), BF16),
-            pltpu.VMEM((2, 4, 48, 128), BF16),
+            pltpu.VMEM((8, 48, 128), BF16),
             pltpu.VMEM((2 * ROWS, 512, 128), BF16),
             pltpu.VMEM((64, 128), F32),
             pltpu.VMEM((4,) + tile, BF16),
@@ -444,21 +452,21 @@
             pltpu.VMEM((128, 1024), F32),
             pltpu.VMEM((1024, 128), F32),
             pltpu.VMEM((4, 16) + tile, BF16),
-            pltpu.VMEM((3, 16) + tile, BF16),
-            pltpu.VMEM((16,) + tile, BF16),
-            pltpu.VMEM((4, 4) + tile, BF16),
+            pltpu.VMEM((4, 3, 4) + tile, BF16),
+            pltpu.VMEM((2, 2) + tile, BF16),
+            pltpu.VMEM((3, 4) + tile, BF16),
+            pltpu.VMEM((12,) + tile, BF16),
             pltpu.VMEM((2 * ROWS, 128, 512), F32),
             pltpu.VMEM((2, 2, 8, 96, 128), F32),
             pltpu.VMEM((2, 8, 96, 128), BF16),
             pltpu.VMEM((2, 8, 96, 128), BF16),
             pltpu.VMEM((2, 8, 96, 128), BF16),
-            pltpu.VMEM((4, 4, 96, 128), BF16),
+            pltpu.VMEM((16, 96, 128), BF16),
             pltpu.VMEM((2 * ROWS, 128, 128), F32),
             pltpu.VMEM((2, 4, 32, 128), BF16),
-            pltpu.VMEM((2, 4, 32, 128), BF16),
+            pltpu.VMEM((8, 32, 128), BF16),
             pltpu.SemaphoreType.REGULAR, sem((6,)), sem((4,)),
-            sem((16,)), sem((16,)), sem((16,)), sem((16,)), sem((8,)), sem((8,)), sem((4,)), sem((4,)), sem((2,)), sem((2,)),
-            sem((4,)), sem((4,)), sem((2,)), sem((8,)), sem((8,)), sem((16,)), sem((16,)), sem((16,)), sem((16,)),
+            sem((2,)), sem((2,)), sem((2,)), sem((2,)), sem((2,)), sem((2,)), sem((2,)), sem((2,)), sem((2,)), sem((2,)), sem((2,)), sem((2,)),
         ],
         compiler_params=pltpu.CompilerParams(
             collective_id=0, has_side_effects=True, vmem_limit_bytes=60 * 1024 * 1024

time: 54 us -> 49.3 us (0.913)
  the two profiles are of different devices: /device:TPU:64 before, /device:TPU:2 now
where the time goes in v4:
time: 49.3 us; the launch traced here: 49.1 us
  Pallas kernels  48.4 us (98%)
  between operations  0.64 us (1%)
    pallas_call x1, Pallas kernels, on_device(): pl.pallas_call(kernel, name='attention_backward', out_shape=shapes, in_sp...  46.9 us
    pallas_call x1, Pallas kernels, on_device(): pl.pallas_call(store, name='store_gradients', out_shape=shapes, in_specs=...  1.55 us

profile of v4, /device:TPU:2, one launch (start us, length us, event | category | flops | bytes accessed | tf_op | source)
XLA Modules:
  0.0 49.1 jit_solution(1687064352533884202)
XLA Ops:
  0.6 46.9 %attention_backward.1 = (bf16[3,64,128]{2,1,0:T(8,128)(2,1)}, bf16[3,64,128]{2,1,0:T(8,128)(2,1)}, bf16[3,64,128]{2,1,0:T(8,128)(2,1)}, f32[4,2,1024]{2,1,0:T(2,128)}) custom-call(bf16[3,64,128]{2,1,0:T(8,128)(2,1)} %q_hbm.1, bf16[3,64,128]{2,1,0:T(8,128)(2,1)} %k_hbm.1, bf16[3,64,128]{2,1,0:T(8,128)(2,1)} %v_hbm.1, s32[3,64]{1,0:T(4,128)} %mask_hbm.1, ...), custom_call_target="tpu_custom_call" | custom-call | tf_op jit(solution)/shard_map/attention_backward/pallas_call | solution.py:423
  47.5 1.5 %store_gradients.1 = (bf16[3,64,128]{2,1,0:T(8,128)(2,1)}, bf16[3,64,128]{2,1,0:T(8,128)(2,1)}, bf16[3,64,128]{2,1,0:T(8,128)(2,1)}, f32[4,2,1024]{2,1,0:T(2,128)}) custom-call(bf16[3,64,128]{2,1,0:T(8,128)(2,1)} %get-tuple-element.8.refs_0_, bf16[3,64,128]{2,1,0:T(8,128)(2,1)} %get-tuple-element.9.refs_1_, bf16[3,64,128]{2,1,0:T(8,128)(2,1)} %get-tuple-element.10.refs_2_, ...), custom_call_target="tpu_custom_call" | custom-call | tf_op jit(solution)/shard_map/store_gradients/pallas_call | solution.py:475

commit v5 on v4

--- a/solution.py
+++ b/solution.py
@@ -42,9 +42,9 @@
     q_hbm, k_hbm, v_hbm, mask_hbm, bias_hbm, do_hbm,
     dq_hbm, dk_hbm, dv_hbm, dbias_hbm,
     dq_ref, dk_ref, dv_ref, dbias_ref, q_ref, k_ref, v_ref, mask_ref, bias_ref, do_ref,
-    swap, kv_send, kv_recv, pen, qd_send, qd_recv, lhs, b_wide, b_send, b_all, b_f32, bias, d_bias,
+    swap, kv_send, kv_recv, pen, qd_send, qd_recv, lhs, b_wide, b_send, b_all, both, stack, b_f32, bias, d_bias,
     d_f32, d_send, d_recv, d_half, d_sum, e_recv, dkv_t, dkv_part, dkv_out, dkv_in, dkv_send, dkv_recv, dq_buf, dq_send, dq_recv,
-    hello, in_sem, out_sem, b1_sem, kv_ss, kv_rs, qd_sem, b2_sem, sh_ss, sh_rs, d2_sem, x_sem, dq_sem, dkv_sem, e_sem,
+    hello, in_sem, out_sem, b1_sem, kv_ss, kv_rs, qd_sem, b2_sem, sh_ss, sh_rs, d2_sem, half_sem, x_sem, dq_sem, dkv_sem, e_sem,
 ):
     r, c = lax.axis_index("row"), lax.axis_index("col")
     z, xl = r // 2, r % 2
@@ -80,7 +80,7 @@
             do(o)
             return carry
 
-        lax.fori_loop(low, high, body, 0)
+        lax.fori_loop(low, high, body, 0, unroll=True)
 
     def arrived(ref, sem):
         pltpu.make_async_remote_copy(
@@ -166,7 +166,7 @@
 
     def b1(o):
         to_y, _, device = yz(o)
-        return copy(b_send.at[to_y], b_all.at[y, z], b1_sem.at[0], b1_sem.at[1], device)
+        return copy(b_send.at[to_y], b_all.at[y, z], b1_sem.at[0], b1_sem.at[1 + o // 4], device)
 
     def kv(o):
         to_y, _, device = yx(o)
@@ -176,14 +176,14 @@
         to_y, to_l, device = yl(o)
         return copy(qd_send.at[to_l, to_y], qd_recv.at[xl * 4 + y], qd_sem.at[0], qd_sem.at[1], device)
 
-    each(1, 12, lambda o: b1(o).start())
+    each(4, 12, lambda o: b1(o).start())
+    each(1, 4, lambda o: b1(o).start())
     each(1, 16, lambda o: kv(o).start())
     each(1, 8, lambda o: qd(o).start())
     b_all[y, z] = b_send[y]
     kv_recv[core, xl, xh * 4 + y] = kv_send[y]
     qd_recv[xl * 4 + y] = qd_send[xl, y]
 
-    arrived(b_all.at[0, pl.ds(0, 11)], b1_sem.at[1])
 
     def block_of(ref, dz, at_z):
         part = {3: pl.ds(0, 2), -3: pl.ds(2, 2)}.get(dz, slice(None))
@@ -193,11 +193,12 @@
         mine = block_of(b_all, dz, z + hop)
         return copy(mine, mine, b2_sem.at[0], b2_sem.at[1], along(dz))
 
-    for hop in hops:
-        for dz in near[:4]:
+    for step, hop in enumerate(hops):
+        arrived(b_all.at[0, pl.ds(0, 4 if step else 3)], b1_sem.at[(1, 3, 2)[step]])
+        if hop:
+            b2(-3 if hop == 5 else 3, hop).start()
+        for dz in (2, -2, 1, -1):
             b2(dz, hop).start()
-    b2(3, -5).start()
-    b2(-3, 5).start()
 
     def share(part):
         slab = kv_recv.at[core, (xl + part) % 2]
@@ -235,6 +236,15 @@
                 seen = seen + kv_recv[g // 2, at_l, (g % 2) * 4 + u, 96:112, :].astype(F32)
             pen[at_l, :, 128 * g:128 * (g + 1)] = 1e9 * (seen - 1.0)
 
+    def keys_of(at):
+        return kv_recv[:, at // ROWS, :, pl.ds(pl.multiple_of(at % ROWS * 32, 32), 32), :].reshape(512, 128)
+
+    def products(at, carry):
+        both[at] = lax.dot_general(lhs[at], keys_of(at), NT, preferred_element_type=F32)
+        return carry
+
+    lax.fori_loop(0, 2 * ROWS, products, 0, unroll=UNROLL)
+
     arrived(b_all.at[:, pl.ds(0, 13)], b2_sem.at[1])
     b_f32[...] = b_all[...].astype(F32).reshape(1024, 128)
     for m in range(8):
@@ -243,12 +253,9 @@
 
     def attention_row(at, carry):
         at_l, i = at // ROWS, at % ROWS
-        left = lhs[at]
-        right = kv_recv[:, at_l, :, pl.ds(pl.multiple_of(i * 32, 32), 32), :].reshape(512, 128)
-        both = lax.dot_general(left, right, NT, preferred_element_type=F32)
-        s_a = both[0:128] * SCALE + bias[:, :512] + pen[at_l, pl.ds(i, 1), :]
-        s_b = both[256:384] * SCALE + bias[:, 512:] + pen[at_l, pl.ds(i + 8, 1), :]
-        dp_a, dp_b = both[128:256], both[384:512]
+        s_a = both[at, 0:128] * SCALE + bias[:, :512] + pen[at_l, pl.ds(i, 1), :]
+        s_b = both[at, 256:384] * SCALE + bias[:, 512:] + pen[at_l, pl.ds(i + 8, 1), :]
+        dp_a, dp_b = both[at, 128:256], both[at, 384:512]
         top = jnp.max(jnp.maximum(s_a, s_b), axis=1, keepdims=True)
         e_a, e_b = jnp.exp(s_a - top), jnp.exp(s_b - top)
         inv = 1.0 / jnp.sum(e_a + e_b, axis=1, keepdims=True)
@@ -257,10 +264,8 @@
         g_a, g_b = p_a * (dp_a - delta_row), p_b * (dp_b - delta_row)
         d_bias[:, :512] += g_a
         d_bias[:, 512:] += g_b
-        g_a, g_b = g_a.astype(BF16), g_b.astype(BF16)
-        stack = jnp.concatenate([g_a, p_a.astype(BF16), g_b, p_b.astype(BF16)], axis=0)
-        dkv_t[at] = lax.dot_general(left, stack, TN, preferred_element_type=F32)
-        dq_buf[at] = (dot(g_a, right) + pltpu.roll(dot(g_b, right), 64, 1)) * SCALE
+        for part, one in enumerate((g_a, p_a, g_b, p_b)):
+            stack[at, 128 * part:128 * (part + 1), :] = one.astype(BF16)
         return carry
 
     lax.fori_loop(0, 2 * ROWS, attention_row, 0, unroll=UNROLL)
@@ -271,13 +276,24 @@
     def d2(dz, hop):
         src = block_of(d_send, {3: -3, -3: 3}.get(dz, dz), z + dz + hop)
         dst = d_recv.at[near.index(dz), hops.index(hop)] if dz in near[:4] else d_half.at[hops.index(hop) - 1]
-        return copy(src, dst, d2_sem.at[0], d2_sem.at[1], along(dz))
+        step = hops.index(hop)
+        arrival = d2_sem.at[1 + step] if dz in near[:4] else half_sem.at[step - 1]
+        return copy(src, dst, d2_sem.at[0], arrival, along(dz))
 
     for hop in hops[::-1]:
-        for dz in near[:4]:
+        if hop:
+            d2(3 if hop == 5 else -3, hop).start()
+        for dz in (2, -2, 1, -1):
             d2(dz, hop).start()
-    d2(3, 5).start()
-    d2(-3, -5).start()
+
+    def row_grads(at, carry):
+        right = keys_of(at)
+        dkv_t[at] = lax.dot_general(lhs[at], stack[at], TN, preferred_element_type=F32)
+        from_b = pltpu.roll(dot(stack[at, 256:384, :], right), 64, 1)
+        dq_buf[at] = (dot(stack[at, 0:128, :], right) + from_b) * SCALE
+        return carry
+
+    lax.fori_loop(0, 2 * ROWS, row_grads, 0, unroll=UNROLL)
 
     for row in range(2 * ROWS):
         for b in range(4):
@@ -320,9 +336,15 @@
     each(1, 16, lambda o: dkv(o).start())
     dkv_recv[x * 4 + y] = dkv_send[xl, xh * 4 + y]
 
-    arrived(d_send.at[:, pl.ds(0, 13)], d2_sem.at[1])
-    for step, hop in enumerate(hops):
-        at_z = (z + hop + 16) % 16
+    def e(o):
+        to_y, step, device = yz(o)
+        return copy(d_sum.at[step, to_y], e_recv.at[y * 3 + step], e_sem.at[0], e_sem.at[1], device)
+
+    for step in (2, 1, 0):
+        at_z = (z + hops[step] + 16) % 16
+        arrived(d_recv.at[:, step], d2_sem.at[1 + step])
+        if step:
+            arrived(d_half.at[step - 1], half_sem.at[step - 1])
         for p in range(4):
             total = d_f32[pl.ds(pl.multiple_of(256 * p + 16 * at_z, 16), 16), :]
             for slot in range(4):
@@ -330,12 +352,7 @@
             if step and p // 2 == 2 - step:
                 total = total + d_half[step - 1, p % 2].astype(F32)
             d_sum[step, p] = total.astype(BF16)
-
-    def e(o):
-        to_y, step, device = yz(o)
-        return copy(d_sum.at[step, to_y], e_recv.at[y * 3 + step], e_sem.at[0], e_sem.at[1], device)
-
-    each(1, 12, lambda o: e(o).start())
+        each(4 * step if step else 1, 4 * step + 4, lambda o: e(o).start())
     e_recv[y * 3] = d_sum[0, y]
 
     arrived(dq_recv.at[pl.ds(0, 7)], dq_sem.at[1])
@@ -447,6 +464,8 @@
             pltpu.VMEM((64, 128), F32),
             pltpu.VMEM((4,) + tile, BF16),
             pltpu.VMEM((4, 16) + tile, BF16),
+            pltpu.VMEM((2 * ROWS, 512, 512), F32),
+            pltpu.VMEM((2 * ROWS, 512, 512), BF16),
             pltpu.VMEM((1024, 128), F32),
             pltpu.VMEM((128, 1024), F32),
             pltpu.VMEM((128, 1024), F32),
@@ -466,7 +485,7 @@
             pltpu.VMEM((2, 4, 32, 128), BF16),
             pltpu.VMEM((8, 32, 128), BF16),
             pltpu.SemaphoreType.REGULAR, sem((6,)), sem((4,)),
-            sem((2,)), sem((2,)), sem((2,)), sem((2,)), sem((2,)), sem((2,)), sem((2,)), sem((2,)), sem((2,)), sem((2,)), sem((2,)), sem((2,)),
+            sem((4,)), sem((2,)), sem((2,)), sem((2,)), sem((2,)), sem((2,)), sem((2,)), sem((4,)), sem((2,)), sem((2,)), sem((2,)), sem((2,)), sem((2,)),
         ],
         compiler_params=pltpu.CompilerParams(
             collective_id=0, has_side_effects=True, vmem_limit_bytes=60 * 1024 * 1024

time: 49.3 us -> 46.1 us (0.935)
  the two profiles are of different devices: /device:TPU:2 before, /device:TPU:1 now
where the time goes in v5:
time: 46.1 us; the launch traced here: 45.9 us
  Pallas kernels  45.2 us (98%)
  between operations  0.64 us (1%)
    pallas_call x1, Pallas kernels, on_device(): pl.pallas_call(kernel, name='attention_backward', out_shape=shapes, in_sp...  43.7 us
    pallas_call x1, Pallas kernels, on_device(): pl.pallas_call(store, name='store_gradients', out_shape=shapes, in_specs=...  1.55 us

profile of v5, /device:TPU:1, one launch (start us, length us, event | category | flops | bytes accessed | tf_op | source)
XLA Modules:
  0.0 45.9 jit_solution(11575206620756136534)
XLA Ops:
  0.6 43.7 %attention_backward.1 = (bf16[3,64,128]{2,1,0:T(8,128)(2,1)}, bf16[3,64,128]{2,1,0:T(8,128)(2,1)}, bf16[3,64,128]{2,1,0:T(8,128)(2,1)}, f32[4,2,1024]{2,1,0:T(2,128)}) custom-call(bf16[3,64,128]{2,1,0:T(8,128)(2,1)} %q_hbm.1, bf16[3,64,128]{2,1,0:T(8,128)(2,1)} %k_hbm.1, bf16[3,64,128]{2,1,0:T(8,128)(2,1)} %v_hbm.1, s32[3,64]{1,0:T(4,128)} %mask_hbm.1, ...), custom_call_target="tpu_custom_call" | custom-call | tf_op jit(solution)/shard_map/attention_backward/pallas_call | solution.py:440
  44.3 1.5 %store_gradients.1 = (bf16[3,64,128]{2,1,0:T(8,128)(2,1)}, bf16[3,64,128]{2,1,0:T(8,128)(2,1)}, bf16[3,64,128]{2,1,0:T(8,128)(2,1)}, f32[4,2,1024]{2,1,0:T(2,128)}) custom-call(bf16[3,64,128]{2,1,0:T(8,128)(2,1)} %get-tuple-element.8.refs_0_, bf16[3,64,128]{2,1,0:T(8,128)(2,1)} %get-tuple-element.9.refs_1_, bf16[3,64,128]{2,1,0:T(8,128)(2,1)} %get-tuple-element.10.refs_2_, ...), custom_call_target="tpu_custom_call" | custom-call | tf_op jit(solution)/shard_map/store_gradients/pallas_call | solution.py:494

commit v6 on v5

--- a/solution.py
+++ b/solution.py
@@ -11,7 +11,6 @@
 ROWS = 3
 UNROLL = 6
 NT = (((1,), (1,)), ((), ()))
-TN = (((0,), (0,)), ((), ()))
 
 
 def iota(shape, dim):
@@ -43,7 +42,7 @@
     dq_hbm, dk_hbm, dv_hbm, dbias_hbm,
     dq_ref, dk_ref, dv_ref, dbias_ref, q_ref, k_ref, v_ref, mask_ref, bias_ref, do_ref,
     swap, kv_send, kv_recv, pen, qd_send, qd_recv, lhs, b_wide, b_send, b_all, both, stack, b_f32, bias, d_bias,
-    d_f32, d_send, d_recv, d_half, d_sum, e_recv, dkv_t, dkv_part, dkv_out, dkv_in, dkv_send, dkv_recv, dq_buf, dq_send, dq_recv,
+    d_f32, d_send, d_recv, d_half, d_sum, e_recv, lhs_t, dkv_part, dkv_out, dkv_in, dkv_send, dkv_recv, dq_buf, dq_send, dq_recv,
     hello, in_sem, out_sem, b1_sem, kv_ss, kv_rs, qd_sem, b2_sem, sh_ss, sh_rs, d2_sem, half_sem, x_sem, dq_sem, dkv_sem, e_sem,
 ):
     r, c = lax.axis_index("row"), lax.axis_index("col")
@@ -241,6 +240,7 @@
 
     def products(at, carry):
         both[at] = lax.dot_general(lhs[at], keys_of(at), NT, preferred_element_type=F32)
+        lhs_t[at] = lhs[at].T
         return carry
 
     lax.fori_loop(0, 2 * ROWS, products, 0, unroll=UNROLL)
@@ -286,23 +286,27 @@
         for dz in (2, -2, 1, -1):
             d2(dz, hop).start()
 
+    def cross(part):
+        return copy(dkv_out.at[part], dkv_in.at[part], x_sem.at[part], x_sem.at[2 + part], sibling)
+
+    for part in range(2):
+        at_l = (xl + part) % 2
+        for i in range(ROWS):
+            at = at_l * ROWS + i
+            grads = dot(lhs_t[at], stack[at])
+            for b in range(4):
+                turned = grads[:, 128 * b:128 * (b + 1)].T.reshape(4, 32, 128)
+                dkv_part[b // 2, at_l, (b % 2) * 4:(b % 2) * 4 + 4, 32 * i:32 * (i + 1), :] = turned
+        dkv_out[part] = dkv_part[1 - core, at_l].astype(BF16)
+        cross(part).start()
+
     def row_grads(at, carry):
         right = keys_of(at)
-        dkv_t[at] = lax.dot_general(lhs[at], stack[at], TN, preferred_element_type=F32)
         from_b = pltpu.roll(dot(stack[at, 256:384, :], right), 64, 1)
         dq_buf[at] = (dot(stack[at, 0:128, :], right) + from_b) * SCALE
         return carry
 
     lax.fori_loop(0, 2 * ROWS, row_grads, 0, unroll=UNROLL)
-
-    for row in range(2 * ROWS):
-        for b in range(4):
-            turned = dkv_t[row, :, 128 * b:128 * (b + 1)].T.reshape(4, 32, 128)
-            i = row % ROWS
-            dkv_part[b // 2, row // ROWS, (b % 2) * 4:(b % 2) * 4 + 4, 32 * i:32 * (i + 1), :] = turned
-    dkv_out[...] = dkv_part[1 - core].astype(BF16)
-    cross = copy(dkv_out, dkv_in, x_sem.at[0], x_sem.at[1], sibling)
-    cross.start()
 
     gather = zero_one(
         ((iota((512, 128), 0) >> 7) * 32 + (iota((512, 128), 0) & 127)) == iota((512, 128), 1)
@@ -325,15 +329,17 @@
     each(1, 8, lambda o: dq(o).start())
     dq_recv[xl * 4 + y] = dq_send[xl, y]
 
-    cross.wait_recv()
-    dkv_send[...] = (dkv_part[core] + dkv_in[...].astype(F32)).astype(BF16)
-
     def dkv(o):
         to_y, to_x, device = yx(o)
         src = dkv_send.at[to_x % 2, (to_x // 2) * 4 + to_y]
         return copy(src, dkv_recv.at[x * 4 + y], dkv_sem.at[0], dkv_sem.at[1], device)
 
-    each(1, 16, lambda o: dkv(o).start())
+    for part in range(2):
+        cross(part).wait_recv()
+        at_l = (xl + part) % 2
+        dkv_send[at_l] = (dkv_part[core, at_l] + dkv_in[part].astype(F32)).astype(BF16)
+        each(4 if part else 1, 8 if part else 4, lambda o: dkv(o).start())
+        each(12 if part else 8, 16 if part else 12, lambda o: dkv(o).start())
     dkv_recv[x * 4 + y] = dkv_send[xl, xh * 4 + y]
 
     def e(o):
@@ -394,7 +400,8 @@
     left(d_send.at[:, pl.ds(0, 13)], d2_sem.at[0])
     for part in range(2):
         share(part).wait_send()
-    cross.wait_send()
+    for part in range(2):
+        cross(part).wait_send()
     left(dq_recv.at[pl.ds(0, 7)], dq_sem.at[0])
     left(dkv_recv.at[pl.ds(0, 15)], dkv_sem.at[0])
     left(e_recv.at[pl.ds(0, 11)], e_sem.at[0])
@@ -475,7 +482,7 @@
             pltpu.VMEM((2, 2) + tile, BF16),
             pltpu.VMEM((3, 4) + tile, BF16),
             pltpu.VMEM((12,) + tile, BF16),
-            pltpu.VMEM((2 * ROWS, 128, 512), F32),
+            pltpu.VMEM((2 * ROWS, 128, 512), BF16),
             pltpu.VMEM((2, 2, 8, 96, 128), F32),
             pltpu.VMEM((2, 8, 96, 128), BF16),
             pltpu.VMEM((2, 8, 96, 128), BF16),
@@ -485,7 +492,7 @@
             pltpu.VMEM((2, 4, 32, 128), BF16),
             pltpu.VMEM((8, 32, 128), BF16),
             pltpu.SemaphoreType.REGULAR, sem((6,)), sem((4,)),
-            sem((4,)), sem((2,)), sem((2,)), sem((2,)), sem((2,)), sem((2,)), sem((2,)), sem((4,)), sem((2,)), sem((2,)), sem((2,)), sem((2,)), sem((2,)),
+            sem((4,)), sem((2,)), sem((2,)), sem((2,)), sem((2,)), sem((2,)), sem((2,)), sem((4,)), sem((2,)), sem((4,)), sem((2,)), sem((2,)), sem((2,)),
         ],
         compiler_params=pltpu.CompilerParams(
             collective_id=0, has_side_effects=True, vmem_limit_bytes=60 * 1024 * 1024

time: 46.1 us -> 45.4 us (0.985)
  Pallas kernels: 45.2 us -> 44.5 us
    pallas_call x1, Pallas kernels: 43.7 us -> 43 us  [on_device(): pl.pallas_call(kernel, name='attention_backward', out_shape=shapes, in_sp...]
where the time goes in v6:
time: 45.4 us; the launch traced here: 45.2 us
  Pallas kernels  44.5 us (98%)
  between operations  0.64 us (1%)
    pallas_call x1, Pallas kernels, on_device(): pl.pallas_call(kernel, name='attention_backward', out_shape=shapes, in_sp...  43 us
    pallas_call x1, Pallas kernels, on_device(): pl.pallas_call(store, name='store_gradients', out_shape=shapes, in_specs=...  1.55 us

profile of v6, /device:TPU:1, one launch (start us, length us, event | category | flops | bytes accessed | tf_op | source)
XLA Modules:
  0.0 45.2 jit_solution(1344636995675751566)
XLA Ops:
  0.6 43.0 %attention_backward.1 = (bf16[3,64,128]{2,1,0:T(8,128)(2,1)}, bf16[3,64,128]{2,1,0:T(8,128)(2,1)}, bf16[3,64,128]{2,1,0:T(8,128)(2,1)}, f32[4,2,1024]{2,1,0:T(2,128)}) custom-call(bf16[3,64,128]{2,1,0:T(8,128)(2,1)} %q_hbm.1, bf16[3,64,128]{2,1,0:T(8,128)(2,1)} %k_hbm.1, bf16[3,64,128]{2,1,0:T(8,128)(2,1)} %v_hbm.1, s32[3,64]{1,0:T(4,128)} %mask_hbm.1, ...), custom_call_target="tpu_custom_call" | custom-call | tf_op jit(solution)/shard_map/attention_backward/pallas_call | solution.py:447
  43.6 1.5 %store_gradients.1 = (bf16[3,64,128]{2,1,0:T(8,128)(2,1)}, bf16[3,64,128]{2,1,0:T(8,128)(2,1)}, bf16[3,64,128]{2,1,0:T(8,128)(2,1)}, f32[4,2,1024]{2,1,0:T(2,128)}) custom-call(bf16[3,64,128]{2,1,0:T(8,128)(2,1)} %get-tuple-element.8.refs_0_, bf16[3,64,128]{2,1,0:T(8,128)(2,1)} %get-tuple-element.9.refs_1_, bf16[3,64,128]{2,1,0:T(8,128)(2,1)} %get-tuple-element.10.refs_2_, ...), custom_call_target="tpu_custom_call" | custom-call | tf_op jit(solution)/shard_map/store_gradients/pallas_call | solution.py:501
